TPU v7x, 256 devices: a whole 4x4x8 slice. The times are simulated.
256 devices in a mesh: ctx: 32 (over x, z_lo, y), state: 8 (over z_hi, core).
Axes of the slice: x: 4, y: 4, z: 8 (z_hi: 4, z_lo: 2; z = z_hi * 2 + z_lo), core: 2. Of those that a mesh axis runs over, the one named last changes fastest.
Arguments:
- key_rows: bfloat16 [12288, 1024], P('ctx'), may hold values from -12 to 12
- value_rows: bfloat16 [12288, 1024], P('ctx'), may hold values from -12 to 12
- token_rates: float32 [12288], P('ctx'), may hold values from 0.1 to 1
- query_rows: bfloat16 [12288, 1024], P('ctx'), may hold values from -6 to 6
- fast_gate: bfloat16 [1024, 12288], P('ctx', 'state'), may hold values from -0.1875 to 0.1875
- fast_up: bfloat16 [1024, 12288], P('ctx', 'state'), may hold values from -0.1875 to 0.1875
- fast_down: bfloat16 [12288, 1024], P('state', 'ctx'), may hold values from -0.0546875 to 0.0546875
Outputs:
- next_out: bfloat16 [12288, 1024], P('ctx', 'state')
All inputs are finite; a program needn't handle non-finite values.
Results may differ from a plain program's by a relative error of at most 0.025.
Values may be sent and summed in bfloat16 or wider, within the bound.
A program may use at most 128 MiB of HBM per device.

v0:
```python
import jax
import jax.numpy as jnp
from jax import lax
from jax.sharding import PartitionSpec as P

epsilon = 1e-06
step_rate = 0.5
contract_first = (((0,), (0,)), ((), ()))
contract_last = (((1,), (1,)), ((), ()))


def swiglu_parts(gate_pre):
    sigmoid_gate = jax.nn.sigmoid(gate_pre)
    return (gate_pre * sigmoid_gate, sigmoid_gate)


def square_sums(matrix, axis_index):
    matrix_float = matrix.astype(jnp.float32)
    return jnp.sum(matrix_float * matrix_float, axis=axis_index)


def on_device(key_rows, value_rows, token_rates, query_rows, fast_gate, fast_up, fast_down):
    gate_full, up_full, down_full = (
        lax.all_gather(fast_gate, "ctx", axis=0, tiled=True),
        lax.all_gather(fast_up, "ctx", axis=0, tiled=True),
        lax.all_gather(fast_down, "ctx", axis=1, tiled=True),
    )
    hidden_width = gate_full.shape[1]
    gate_pre = jnp.dot(key_rows, gate_full, preferred_element_type=jnp.float32)
    up_pre = jnp.dot(key_rows, up_full, preferred_element_type=jnp.float32)
    silu_gate, sigmoid_gate = swiglu_parts(gate_pre)
    hidden = (silu_gate * up_pre).astype(jnp.bfloat16)
    target = (value_rows.astype(jnp.float32) * token_rates[:, None]).astype(jnp.bfloat16)
    back_grad = lax.dot_general(
        target, down_full, contract_last, preferred_element_type=jnp.float32
    )
    grad_gate = (
        back_grad * up_pre * sigmoid_gate * (1.0 + gate_pre * (1.0 - sigmoid_gate))
    ).astype(jnp.bfloat16)
    grad_up = (back_grad * silu_gate).astype(jnp.bfloat16)
    direction = lax.psum_scatter(
        jnp.concatenate(
            [
                lax.dot_general(
                    key_rows, grad_gate, contract_first, preferred_element_type=jnp.float32
                ),
                lax.dot_general(
                    key_rows, grad_up, contract_first, preferred_element_type=jnp.float32
                ),
                lax.dot_general(target, hidden, contract_first, preferred_element_type=jnp.float32),
            ],
            axis=1,
        ).astype(jnp.bfloat16),
        "ctx",
        scatter_dimension=0,
        tiled=True,
    ).astype(jnp.float32)
    own_rows = jnp.concatenate([fast_gate, fast_up, fast_down.T], axis=1).astype(jnp.float32)
    weight_sq = jnp.concatenate(
        [square_sums(gate_full, 0), square_sums(up_full, 0), square_sums(down_full, 1)]
    )
    weight_norm = jnp.sqrt(weight_sq + epsilon)
    direction_sq = lax.psum(jnp.sum(direction * direction, axis=0), "ctx")
    stepped = own_rows + step_rate * weight_norm / jnp.sqrt(direction_sq + epsilon) * direction
    stepped_sq = lax.psum(jnp.sum(stepped * stepped, axis=0), "ctx")
    renewed = (stepped * (weight_norm / jnp.sqrt(stepped_sq + epsilon))).astype(jnp.bfloat16)
    renewed_full = lax.all_gather(renewed, "ctx", axis=0, tiled=True)
    gate_next = jnp.dot(
        query_rows, renewed_full[:, :hidden_width], preferred_element_type=jnp.float32
    )
    up_next = jnp.dot(
        query_rows,
        renewed_full[:, hidden_width : 2 * hidden_width],
        preferred_element_type=jnp.float32,
    )
    silu_next, sigmoid_next = swiglu_parts(gate_next)
    hidden_next = (silu_next * up_next).astype(jnp.bfloat16)
    out_terms = lax.dot_general(
        hidden_next,
        renewed_full[:, 2 * hidden_width :],
        contract_last,
        preferred_element_type=jnp.float32,
    )
    return lax.psum_scatter(
        out_terms.astype(jnp.bfloat16), "state", scatter_dimension=1, tiled=True
    )


def solution(mesh):
    placed = (
        P("ctx", None),
        P("ctx", None),
        P("ctx"),
        P("ctx", None),
        P("ctx", "state"),
        P("ctx", "state"),
        P("state", "ctx"),
    )
    return jax.shard_map(
        on_device, mesh=mesh, in_specs=placed, out_specs=P("ctx", "state"), check_vma=False
    )
```

profile of v0, /device:TPU:8, one launch (start us, length us, event | category | flops | bytes accessed | tf_op | source)
XLA Modules:
  0.0 1233.2 jit_solution(7628328202828484660)
XLA Ops:
  6.5 0.0 copy-start
  6.5 0.0 all-gather.5.cloned.1.call-start
  6.5 0.7 all-gather.5.cloned.1.call-update
  7.3 0.0 all-gather.9.cloned.1.call-start
  7.3 0.7 all-gather.9.cloned.1.call-update
  8.0 0.0 all-gather.7.cloned.1.call-start
  8.1 0.7 all-gather.7.cloned.1.call-update
  8.7 0.0 copy-start.7
  8.8 0.0 copy-start.9
  8.8 0.0 reduce-scatter.7.cloned.1.call-start
  8.8 160.9 %all-gather.5.cloned.1.call-done = bf16[1024,1536]{1,0:T(8,128)(2,1)} async-done(((bf16[32,1536]{1,0:T(8,128)(2,1)}), bf16[1024,1536]{1,0:T(8,128)(2,1)}) %all-gather.5.cloned.1.call-update) | async-done | bytes 3145744 | tf_op jit(solution)/shard_map/all_gather | solution.py:24
  169.7 4.7 fusion.40
  174.5 154.2 %all-gather.9.cloned.1.call-done = bf16[1536,1024]{0,1:T(8,128)(2,1)} async-done(((bf16[1536,32]{0,1:T(8,128)(2,1)}), bf16[1536,1024]{0,1:T(8,128)(2,1)}) %all-gather.9.cloned.1.call-update) | async-done | bytes 3145744 | tf_op jit(solution)/shard_map/all_gather | solution.py:26
  328.7 0.0 copy-done.9
  328.7 3.5 fusion.33
  332.2 1.4 copy-done.10
  333.6 3.6 fusion.1
  337.1 150.5 %all-gather.7.cloned.1.call-done = bf16[1024,1536]{1,0:T(8,128)(2,1)} async-done(((bf16[32,1536]{1,0:T(8,128)(2,1)}), bf16[1024,1536]{1,0:T(8,128)(2,1)}) %all-gather.7.cloned.1.call-update) | async-done | bytes 3145744 | tf_op jit(solution)/shard_map/all_gather | solution.py:25
  487.6 3.4 fusion.39
  491.1 0.0 copy-done.11
  491.1 0.0 copy-done.13
  491.1 2.3 fusion
  493.4 2.1 convolution_convert_fusion
  495.5 4.4 pad_maximum_fusion
  499.9 12.8 %copy.24 = bf16[1024,4608]{1,0:T(8,128)(2,1)} copy(bf16[1024,4608]{0,1:T(8,128)(2,1)} %pad_maximum_fusion) | data formatting | bytes 18874368
  512.7 0.0 reduce-scatter.7.cloned.1.call-update
  512.7 0.2 all-gather.11.cloned.1.call-start
  512.9 0.0 copy-start.2
  512.9 2.7 multiply_reduce_fusion.1
  515.6 0.1 copy-done.2
  515.8 0.7 multiply_reduce_fusion.2
  516.4 1.2 copy-done.3
  517.7 0.7 multiply_reduce_fusion
  518.3 174.6 %reduce-scatter.7.cloned.1.call-done = bf16[32,4608]{1,0:T(8,128)(2,1)} async-done(((bf16[1024,4608]{1,0:T(8,128)(2,1)}), bf16[32,4608]{1,0:T(8,128)(2,1)}) %reduce-scatter.7.cloned.1.call-update) | async-done | bytes 294928 | tf_op jit(solution)/shard_map/reduce_scatter | solution.py:41
  692.9 1.1 fusion.29
  694.0 151.9 %psum.14 = f32[4608]{0:T(1024)S(1)} all-reduce(f32[4608]{0:T(1024)S(1)} %fusion.29), channel_id=1, replica_groups=mesh['ctx'=32,'state'=8] {'ctx'}, use_global_device_ids=true, to_apply=%region_5.0 | all-reduce | flops 4608 | bytes 36864 | tf_op jit(solution)/shard_map/psum | solution.py:63
  845.9 1.1 multiply_reduce_fusion.3
  847.0 154.3 %psum.15 = f32[4608]{0:T(1024)S(1)} all-reduce(f32[4608]{0:T(1024)S(1)} %multiply_reduce_fusion.3), channel_id=1, replica_groups=mesh['ctx'=32,'state'=8] {'ctx'}, use_global_device_ids=true, to_apply=%region_7.0 | all-reduce | flops 4608 | bytes 36864 | tf_op jit(solution)/shard_map/psum | solution.py:65
  1001.3 1.8 multiply_convert_fusion.7
  1003.1 0.0 all-gather.11.cloned.1.call-update
  1003.1 0.0 reduce-scatter.9.cloned.1.call-start
  1003.2 169.6 %all-gather.11.cloned.1.call-done = bf16[1024,4608]{1,0:T(8,128)(2,1)} async-done(((bf16[32,4608]{1,0:T(8,128)(2,1)}), bf16[1024,4608]{1,0:T(8,128)(2,1)}) %all-gather.11.cloned.1.call-update) | async-done | bytes 9437200 | tf_op jit(solution)/shard_map/all_gather | solution.py:67
  1172.8 4.7 fusion.8
  1177.5 6.2 fusion.23
  1183.7 1.2 copy.26
  1184.8 0.0 reduce-scatter.9.cloned.1.call-update
  1184.9 39.9 %reduce-scatter.9.cloned.1.call-done = bf16[128,384]{1,0:T(8,128)(2,1)} async-done(((bf16[1024,384]{1,0:T(8,128)(2,1)}), bf16[128,384]{1,0:T(8,128)(2,1)}) %reduce-scatter.9.cloned.1.call-update) | async-done | bytes 98320
  1224.7 1.6 copy.27
  (20 shorter events, 0.1 us)
Async XLA Ops:
  6.5 163.2 %copy-start = (bf16[384,1024]{1,0:T(8,128)(2,1)S(1)}, bf16[384,1024]{1,0:T(8,128)(2,1)}, u32[]{:S(2)}) copy-start(bf16[384,1024]{1,0:T(8,128)(2,1)} %param.7) | copy-start | bytes 2359300
  6.5 163.2 %all-gather.5.cloned.1.call-start = ((), (), s32[]{:S(2)}) async-start(), calls=%async_computation.2 | async-start | bytes 3244032 | tf_op jit(solution)/shard_map/all_gather | solution.py:24
  7.3 321.4 %all-gather.9.cloned.1.call-start = ((), (), s32[]{:S(2)}) async-start(), calls=%async_computation.4 | async-start | bytes 3244032 | tf_op jit(solution)/shard_map/all_gather | solution.py:26
  8.0 479.6 %all-gather.7.cloned.1.call-start = ((), (), s32[]{:S(2)}) async-start(), calls=%async_computation.3 | async-start | bytes 3244032 | tf_op jit(solution)/shard_map/all_gather | solution.py:25
  8.7 319.9 %copy-start.7 = (bf16[384,1024]{1,0:T(8,128)(2,1)S(1)}, bf16[384,1024]{1,0:T(8,128)(2,1)}, u32[]{:S(2)}) copy-start(bf16[384,1024]{1,0:T(8,128)(2,1)} %param.8) | copy-start | bytes 2359300
  8.8 319.9 %copy-start.9 = (f32[384]{0:T(512)S(1)}, f32[384]{0:T(512)}, u32[]{:S(2)}) copy-start(f32[384]{0:T(512)} %param.9) | copy-start | bytes 4612
  8.8 684.2 %reduce-scatter.7.cloned.1.call-start = ((), (), s32[]{:S(2)}) async-start(), calls=%async_computation.6 | async-start | bytes 9732096 | tf_op jit(solution)/shard_map/reduce_scatter | solution.py:41
  328.7 4.9 copy-start.12
  332.2 1.4 copy-start.10
  487.6 3.4 copy-start.11
  487.6 3.4 copy-start.13
  493.4 2.1 copy-start.1
  512.7 660.1 %all-gather.11.cloned.1.call-start = ((), (), s32[]{:S(2)}) async-start(), calls=%async_computation.5 | async-start | bytes 9732096 | tf_op jit(solution)/shard_map/all_gather | solution.py:67
  512.9 2.8 copy-start.2
  515.8 1.9 copy-start.3
  517.6 328.2 %copy-start.4 = (bf16[32,1536]{1,0:T(8,128)(2,1)S(1)}, bf16[32,1536]{1,0:T(8,128)(2,1)}, u32[]{:S(2)}) copy-start(bf16[32,1536]{1,0:T(8,128)(2,1)} %param.11) | copy-start | bytes 294916
  517.7 328.2 %copy-start.5 = (bf16[1536,32]{0,1:T(8,128)(2,1)S(1)}, bf16[1536,32]{0,1:T(8,128)(2,1)}, u32[]{:S(2)}) copy-start(bf16[1536,32]{0,1:T(8,128)(2,1)} %param.13) | copy-start | bytes 294916
  517.7 328.2 %copy-start.6 = (bf16[32,1536]{1,0:T(8,128)(2,1)S(1)}, bf16[32,1536]{1,0:T(8,128)(2,1)}, u32[]{:S(2)}) copy-start(bf16[32,1536]{1,0:T(8,128)(2,1)} %param.12) | copy-start | bytes 294916
  517.7 655.2 %copy-start.8 = (bf16[384,1024]{1,0:T(8,128)(2,1)S(1)}, bf16[384,1024]{1,0:T(8,128)(2,1)}, u32[]{:S(2)}) copy-start(bf16[384,1024]{1,0:T(8,128)(2,1)} %param.10) | copy-start | bytes 2359300
  1003.1 221.6 %reduce-scatter.9.cloned.1.call-start = ((), (), s32[]{:S(2)}) async-start(), calls=%async_computation.7 | async-start | bytes 884736
Sparse Core Ops, SparseCore 0:
  9.1 160.5 all-gather.4
  171.5 157.1 all-gather.8
  330.5 157.1 all-gather.6
  512.8 180.0 reduce-scatter.6
  1003.3 169.4 all-gather.10
  1185.0 39.6 reduce-scatter.8
where the time goes:
time: 1230 us
  waiting for transfers between devices  852 us (69%)
  blocking collectives  306 us (25%)
  matrix products  30.4 us (2%)
  local copies, waits for them, and re-layouts  18.3 us (1%)
  between operations  13.6 us (1%)
  other arithmetic  12.5 us (1%)
    reduce_scatter x1, waiting for transfers between devices, on_device(): lax.psum_scatter(jnp.concatenate([lax.dot_general(key_rows, grad_gate, co...  175 us
    all_gather x1, waiting for transfers between devices, on_device(): renewed_full = lax.all_gather(renewed, 'ctx', axis=0, tiled=True)  170 us
    all_gather x1, waiting for transfers between devices, on_device(): lax.all_gather(fast_gate, 'ctx', axis=0, tiled=True)  161 us
    psum x1, blocking collectives, on_device(): stepped_sq = lax.psum(jnp.sum(stepped * stepped, axis=0), 'ctx')  154 us
    all_gather x1, waiting for transfers between devices, on_device(): lax.all_gather(fast_down, 'ctx', axis=1, tiled=True)  154 us
    psum x1, blocking collectives, on_device(): direction_sq = lax.psum(jnp.sum(direction * direction, axis=0), 'ctx')  152 us
    all_gather x1, waiting for transfers between devices, on_device(): lax.all_gather(fast_up, 'ctx', axis=0, tiled=True)  151 us
    unnamed x7, waiting for transfers between devices  42 us
  transfers between devices with their start and end apart: 6, of which 6 were waited for; matrix products, arithmetic and copies ran while one was open for 1% of the time, Pallas kernels for 0%

commit v1 on v0

v1 whole, which is shorter than its diff:
```python
import functools

import jax
import jax.numpy as jnp
from jax import lax
from jax.experimental import pallas as pl
from jax.experimental.pallas import tpu as pltpu
from jax.sharding import PartitionSpec as P

MESH = pl.DeviceIdType.MESH
EPS = 1e-06
RATE = 0.5
NT = (((1,), (1,)), ((), ()))
NN = (((1,), (0,)), ((), ()))
F32, BF16 = jnp.float32, jnp.bfloat16
N_SEM = 160


def dot(a, b, dims):
    return lax.dot_general(a, b, dims, preferred_element_type=F32)


def place(x, y, z, k):
    return (x * 8 + (z % 2) * 4 + y, (z // 2) * 2 + k)


class Links:
    def __init__(self, send_sem, recv_sem):
        self.send_sem, self.recv_sem, self.used, self.sent = send_sem, recv_sem, 0, []

    def ids(self, count=1):
        first = self.used
        self.used += count
        assert self.used <= N_SEM
        return first

    def send(self, index, src, dst, device):
        copy = pltpu.make_async_remote_copy(
            src_ref=src, dst_ref=dst, send_sem=self.send_sem.at[index], recv_sem=self.recv_sem.at[index],
            device_id=device, device_id_type=MESH)
        copy.start()
        self.sent.append(copy)

    def wait(self, index, dst, device):
        pltpu.make_async_remote_copy(
            src_ref=dst, dst_ref=dst, send_sem=self.send_sem.at[index], recv_sem=self.recv_sem.at[index],
            device_id=device, device_id_type=MESH).wait_recv()

    def drain(self):
        for copy in self.sent:
            copy.wait_send()


def kernel(key_ref, val_ref, rate_ref, qry_ref, gate_ref, up_ref, down_ref, out_ref,
           key_all, val_all, qry_all, rates, quarter, w, gp, uq, hid, grads,
           d, ry0, x1a0, x1b0, x2a0, x2b0, x1a, x1b, x2a, x2b, e, es, ry, new,
           ob, osib, r, ryo, za0, zb0, za, zb, ya0, yb0, ya, ybuf, fin, fins, yfin,
           send_sem, recv_sem, local_sem):
    c, s = lax.axis_index("ctx"), lax.axis_index("state")
    x, zlo, y = c // 8, (c // 4) % 2, c % 4
    zhi, k = s // 2, s % 2
    z = 2 * zhi + zlo
    p, yb = y // 2, y % 2
    xp, xm, xo = (x + 1) % 4, (x + 3) % 4, (x + 2) % 4
    zp, zm = (z + 1) % 8, (z + 7) % 8
    yt = y + 1 - 2 * yb
    yr = 3 - y
    po = 1 - p
    links = Links(send_sem, recv_sem)
    dev_xp, dev_xm = place(xp, y, z, k), place(xm, y, z, k)
    dev_yt, dev_yr = place(x, yt, z, k), place(x, yr, z, k)
    dev_zp, dev_zm = place(x, y, zp, k), place(x, y, zm, k)
    dev_core = place(x, y, z, 1 - k)
    z_pair = z + 1 - 2 * zlo
    z_other = jnp.where(zlo == 0, zm, zp)

    def block(yy, zz):
        return 2 * yy + zz

    me = block(yb, zlo)

    full = [key_all, val_all, qry_all]
    src = [key_ref, val_ref, qry_ref]
    local = []
    for i in range(3):
        copy = pltpu.make_async_copy(
            src[i], full[i].at[pl.ds(pl.multiple_of(me * 384, 16), 384)], local_sem.at[i])
        copy.start()
        local.append(copy)

    barrier = pltpu.get_barrier_semaphore()
    for dy in range(4):
        for dz in range(2):
            if dy or dz:
                pl.semaphore_signal(barrier, inc=1, device_id=place(x, (y + dy) % 4, 2 * zhi + (zlo + dz) % 2, k), device_id_type=MESH)
    for other in (dev_xp, dev_xm, place(x, y, z_other, k), dev_core):
        pl.semaphore_signal(barrier, inc=1, device_id=other, device_id_type=MESH)
    pl.semaphore_wait(barrier, 11)

    first = links.ids(12)
    weights = [gate_ref, up_ref, down_ref]
    stage = []
    for a in range(3):
        for qz in range(2):
            for q2 in range(2):
                ty = jnp.where(zlo == 0, q2, 3 - q2)
                own = jnp.logical_and(ty == y, zlo == qz)
                piece = weights[a].at[:, pl.ds((qz * 2 + q2) * 384, 384)]
                into = quarter.at[a, pl.ds(pl.multiple_of(32 * y, 32), 32)]
                copy = pltpu.make_async_remote_copy(
                    src_ref=piece, dst_ref=into, send_sem=send_sem.at[first + a * 4 + qz * 2 + q2],
                    recv_sem=recv_sem.at[first + a * 4 + y],
                    device_id=place(x, ty, 2 * zhi + qz, k), device_id_type=MESH)
                stay = pltpu.make_async_copy(piece, into, local_sem.at[3 + a])
                stage.append((own, copy, stay))

                @pl.when(own)
                def _():
                    stay.start()

                @pl.when(jnp.logical_not(own))
                def _():
                    copy.start()

    rate_id = links.ids(3)

    def rate_at(b):
        return rates.at[:, pl.ds(pl.multiple_of(b * 384, 128), 384)]

    rate_copy = pltpu.make_async_copy(rate_ref, rate_at(me), local_sem.at[6])
    rate_copy.start()
    links.send(rate_id, rate_ref, rate_at(me), dev_yt)
    links.send(rate_id + 1, rate_ref, rate_at(me), place(x, y, z_pair, k))
    links.send(rate_id + 2, rate_ref, rate_at(me), place(x, yt, z_pair, k))

    blocks = {"a": block(1 - yb, zlo), "b": block(yb, 1 - zlo), "c": block(1 - yb, 1 - zlo)}
    tok_ids = {(i, kind, h): links.ids() for i in range(3) for kind in "abc" for h in range(2)}
    sib_ids = {(i, kind, h): links.ids() for i in range(3) for kind in "abc" for h in range(2)}

    def rows(i, b, h, kk=k):
        return full[i].at[pl.ds(pl.multiple_of(b * 384 + kk * 192 + h * 96, 16), 96)]

    z_to = [dev_zp, dev_zm]

    def token_start(i):
        for h in range(2):
            mine = src[i].at[pl.ds(pl.multiple_of(k * 192 + h * 96, 16), 96)]
            links.send(tok_ids[i, "a", h], mine, rows(i, me, h), dev_yt)
            links.send(tok_ids[i, "b", h], mine, rows(i, me, h), z_to[h])

    def token_pass(i, kind):
        for h in range(2):
            here = rows(i, blocks[kind], h)
            links.wait(tok_ids[i, kind, h], here, dev_core)
            if kind == "a":
                links.send(tok_ids[i, "c", h], here, here, z_to[h])
            links.send(sib_ids[i, kind, h], here, here, dev_core)

    def token_finish(i):
        for kind in "abc":
            for h in range(2):
                links.wait(sib_ids[i, kind, h], rows(i, blocks[kind], h, 1 - k), dev_core)

    def gather(piece, half):
        base = {name: links.ids(3) for name in ("xp", "xm", "y", "fp", "fm", "xp2", "xm2", "fp2", "fm2", "y1", "y2", "y3")}

        def start(a):
            links.send(base["xp"] + a, piece(a, x, p), piece(a, x, p), dev_xp)
            links.send(base["xm"] + a, piece(a, x, p), piece(a, x, p), dev_xm)
            links.send(base["y"] + a, piece(a, x, p), piece(a, x, p), dev_yr)

        def cross(a):
            links.wait(base["y"] + a, piece(a, x, po), dev_yr)
            links.send(base["xp2"] + a, piece(a, x, po), piece(a, x, po), dev_xp)
            links.send(base["xm2"] + a, piece(a, x, po), piece(a, x, po), dev_xm)

        def onward(a, which, pp):
            links.wait(base["xp" + which] + a, piece(a, xm, pp), dev_xm)
            links.send(base["fp" + which] + a, half(a, xm, pp, 0), half(a, xm, pp, 0), dev_xp)
            if a == 0:
                links.send(base["y1"], piece(a, xm, pp), piece(a, xm, pp), dev_yr)
            links.wait(base["xm" + which] + a, piece(a, xp, pp), dev_xp)
            links.send(base["fm" + which] + a, half(a, xp, pp, 1), half(a, xp, pp, 1), dev_xm)
            if a == 0:
                links.send(base["y2"], piece(a, xp, pp), piece(a, xp, pp), dev_yr)

        def far(a, which, pp):
            links.wait(base["fp" + which] + a, half(a, xo, pp, 0), dev_xm)
            links.wait(base["fm" + which] + a, half(a, xo, pp, 1), dev_xp)
            if a == 0:
                links.send(base["y3"], piece(a, xo, pp), piece(a, xo, pp), dev_yr)

        def finish(a):
            if a == 0:
                links.wait(base["y"], piece(a, x, po), dev_yr)
                links.wait(base["y1"], piece(a, xm, po), dev_yr)
                links.wait(base["y2"], piece(a, xp, po), dev_yr)
                links.wait(base["y3"], piece(a, xo, po), dev_yr)
            else:
                far(a, "2", po)

        return start, cross, onward, far, finish

    def w_piece(a, xx, pp):
        return w.at[a, :, pl.ds(pl.multiple_of((2 * xx + pp) * 128, 128), 128)]

    def w_half(a, xx, pp, h):
        return w.at[a, pl.ds(192 * h, 192), pl.ds(pl.multiple_of((2 * xx + pp) * 128, 128), 128)]

    token_start(0)
    w_start, w_cross, w_onward, w_far, w_finish = gather(w_piece, w_half)
    for a in range(3):
        for own, copy, stay in stage[4 * a:4 * a + 4]:
            @pl.when(own)
            def _():
                stay.wait()

        for ys in range(4):
            @pl.when(jnp.logical_or(ys != y, zlo != p))
            def _():
                links.wait(first + a * 4 + ys, quarter.at[a, pl.ds(32 * ys, 32)], dev_core)
        w_piece(a, x, p)[...] = quarter[a].astype(F32).T.astype(BF16)
        w_start(a)
    token_start(1)
    token_pass(0, "b")
    token_pass(0, "a")
    w_cross(1)
    w_cross(2)
    w_onward(0, "", p)
    w_onward(1, "", p)
    token_pass(0, "c")
    token_pass(1, "b")
    token_pass(1, "a")
    w_onward(2, "", p)
    w_far(0, "", p)
    w_onward(1, "2", po)
    w_onward(2, "2", po)
    token_start(2)
    token_pass(1, "c")
    for copy in local:
        copy.wait()
    rate_copy.wait()
    for i, b in enumerate(("a", "b", "c")):
        links.wait(rate_id + i, rate_at(blocks[b]), dev_core)
    token_finish(0)
    w_finish(0)
    w_far(1, "", p)
    w_finish(1)

    def forward(t, carry):
        cols = pl.ds(pl.multiple_of(t * 512, 512), 512)
        keys = key_all[cols, :]
        gate_pre = dot(w[0], keys, NT)
        up_pre = dot(w[1], keys, NT)
        gp[:, cols] = gate_pre
        uq[:, cols] = up_pre
        hid[:, cols] = (gate_pre * jax.nn.sigmoid(gate_pre) * up_pre * rates[:, cols]).astype(BF16)
        return carry

    lax.fori_loop(0, 3, forward, 0)
    token_finish(1)

    def direction(a, acts, tokens):
        def part(n, carry):
            cols = pl.ds(pl.multiple_of(n * 256, 256), 256)
            term = dot(acts[...], tokens[:, cols], NN)
            d[a, :, :, :, cols] = term.reshape(4, 2, 48, 256).astype(BF16)
            return carry
        lax.fori_loop(0, 4, part, 0)

    rs = {name: links.ids(3) for name in ("ap", "bm", "p", "m", "y")}
    ab = [pl.ds(0, 512), pl.ds(512, 512)]

    def reduce_start(a):
        links.send(rs["ap"] + a, d.at[a, xo, :, :, ab[0]], x1a.at[a - 1], dev_xp)
        links.send(rs["bm"] + a, d.at[a, xo, :, :, ab[1]], x1b.at[a - 1], dev_xm)

    def reduce_merge(a):
        links.wait(rs["ap"] + a, x1a.at[a - 1], dev_xm)
        d[a, xp, :, :, ab[0]] = (d[a, xp, :, :, ab[0]].astype(F32) + x1a[a - 1].astype(F32)).astype(BF16)
        links.send(rs["p"] + a, d.at[a, xp], x2a.at[a - 1], dev_xp)
        links.wait(rs["bm"] + a, x1b.at[a - 1], dev_xp)
        d[a, xm, :, :, ab[1]] = (d[a, xm, :, :, ab[1]].astype(F32) + x1b[a - 1].astype(F32)).astype(BF16)
        links.send(rs["m"] + a, d.at[a, xm], x2b.at[a - 1], dev_xm)

    def reduce_cross(a):
        links.wait(rs["p"] + a, x2a.at[a - 1], dev_xm)
        links.wait(rs["m"] + a, x2b.at[a - 1], dev_xp)
        total = d[a, x].astype(F32) + x2a[a - 1].astype(F32) + x2b[a - 1].astype(F32)
        e[a - 1] = total
        es[a - 1] = total.astype(BF16)
        links.send(rs["y"] + a, es.at[a - 1, po], ry.at[a - 1], dev_yr)

    def renew(a, grad):
        unit = pl.ds(pl.multiple_of((2 * x + p) * 48, 16), 48)
        old = w[a, unit, :].astype(F32)
        norm = jnp.sqrt(jnp.sum(old * old, axis=1, keepdims=True) + EPS)
        stepped = old + RATE * norm / jnp.sqrt(jnp.sum(grad * grad, axis=1, keepdims=True) + EPS) * grad
        scale = norm / jnp.sqrt(jnp.sum(stepped * stepped, axis=1, keepdims=True) + EPS)
        new[a, x, p] = (stepped * scale).astype(BF16)

    direction(2, hid, val_all)
    reduce_start(2)
    w_far(2, "", p)
    w_finish(2)

    def backward(t, carry):
        cols = pl.ds(pl.multiple_of(t * 512, 512), 512)
        back = dot(w[2], val_all[cols, :], NT) * rates[:, cols]
        gate_pre, up_pre = gp[:, cols], uq[:, cols]
        sig = jax.nn.sigmoid(gate_pre)
        grads[0, :, cols] = (back * up_pre * sig * (1.0 + gate_pre * (1.0 - sig))).astype(BF16)
        grads[1, :, cols] = (back * gate_pre * sig).astype(BF16)
        return carry

    lax.fori_loop(0, 3, backward, 0)
    direction(0, grads.at[0], key_all)
    links.send(rs["y"], d.at[0, :, po], ry0, dev_yr)
    direction(1, grads.at[1], key_all)
    reduce_start(1)
    reduce_merge(2)
    links.wait(rs["y"], ry0, dev_yr)
    d[0, :, p] = (d[0, :, p].astype(F32) + ry0[...].astype(F32)).astype(BF16)
    links.send(rs["ap"], d.at[0, xo, p, :, ab[0]], x1a0, dev_xp)
    links.send(rs["bm"], d.at[0, xo, p, :, ab[1]], x1b0, dev_xm)
    reduce_merge(1)
    token_pass(2, "b")
    token_pass(2, "a")
    links.wait(rs["ap"], x1a0, dev_xm)
    d[0, xp, p, :, ab[0]] = (d[0, xp, p, :, ab[0]].astype(F32) + x1a0[...].astype(F32)).astype(BF16)
    links.send(rs["p"], d.at[0, xp, p], x2a0, dev_xp)
    links.wait(rs["bm"], x1b0, dev_xp)
    d[0, xm, p, :, ab[1]] = (d[0, xm, p, :, ab[1]].astype(F32) + x1b0[...].astype(F32)).astype(BF16)
    links.send(rs["m"], d.at[0, xm, p], x2b0, dev_xm)
    reduce_cross(2)
    reduce_cross(1)
    token_pass(2, "c")

    def n_piece(a, xx, pp):
        return new.at[a, xx, pp]

    def n_half(a, xx, pp, h):
        return new.at[a, xx, pp, :, ab[h]]

    n_start, n_cross, n_onward, n_far, n_finish = gather(n_piece, n_half)
    links.wait(rs["p"], x2a0, dev_xm)
    links.wait(rs["m"], x2b0, dev_xp)
    renew(0, d[0, x, p].astype(F32) + x2a0[...].astype(F32) + x2b0[...].astype(F32))
    n_start(0)
    for a in (2, 1):
        links.wait(rs["y"] + a, ry.at[a - 1], dev_yr)
        renew(a, e[a - 1, p] + ry[a - 1].astype(F32))
        n_start(a)
    n_onward(0, "", p)
    n_cross(2)
    n_cross(1)
    n_onward(2, "", p)
    n_onward(1, "", p)
    n_far(0, "", p)
    n_onward(2, "2", po)
    n_onward(1, "2", po)
    n_far(2, "", p)
    n_far(1, "", p)
    token_finish(2)
    n_finish(0)
    n_finish(1)
    n_finish(2)

    core_ids = links.ids(4)

    def apply(b, carry):
        q = qry_all[pl.ds(pl.multiple_of(b * 384, 16), 384), :]
        gate_next = dot(q, new[0].reshape(384, 1024), NT)
        up_next = dot(q, new[1].reshape(384, 1024), NT)
        act = (gate_next * jax.nn.sigmoid(gate_next) * up_next).astype(BF16)
        term = dot(act, new[2].reshape(384, 1024), NN)
        for zz in range(4):
            for kk in range(2):
                at = (2 * zz + kk) * 128
                ob[b, kk, zz] = term[:, at:at + 128].astype(BF16)
        return carry

    for b in range(4):
        apply(b, 0)
        links.send(core_ids + b, ob.at[b, 1 - k], osib.at[b], dev_core)
    for b in range(4):
        links.wait(core_ids + b, osib.at[b], dev_core)
        r[b // 2, b % 2] = (ob[b, k].astype(F32) + osib[b].astype(F32)).astype(BF16)

    lo, hi = pl.ds(0, 192), pl.ds(192, 192)
    y_id = links.ids()
    links.send(y_id, r.at[1 - yb, :, :, lo], ryo, dev_yt)
    ring = {name: links.ids(4) for name in ("zp", "zm", "yp", "ym")}

    def at(step, sign):
        t = (z + sign * (4 - step) + 8) % 8
        return t % 2, t // 2

    def chunk(kind, t, part):
        if kind == "z":
            return (slice(None), t[0], t[1], pl.ds(192 + part[0], part[1]))
        return (yb, t[0], t[1], pl.ds(part[0], part[1]))

    halves = {1: (0, 96), -1: (96, 96)}
    slots = {("z", 1): (za0, za), ("z", -1): (zb0, zb), ("y", 1): (ya0, ya), ("y", -1): (yb0, ybuf)}

    def slot(kind, sign, step):
        return slots[kind, sign][0] if step == 0 else slots[kind, sign][1].at[step - 1]

    def ring_send(kind, sign, step):
        part = halves[sign] if step == 0 else (0, 192)
        links.send(ring[kind + ("p" if sign > 0 else "m")] + step, r.at[chunk(kind, at(step, sign), part)],
                   slot(kind, sign, step), dev_zp if sign > 0 else dev_zm)

    def ring_recv(kind, sign, step):
        got = slot(kind, sign, step)
        links.wait(ring[kind + ("p" if sign > 0 else "m")] + step, got, dev_zm if sign > 0 else dev_zp)
        return got

    def ring_add(kind, sign, step):
        got = ring_recv(kind, sign, step)
        where = chunk(kind, at(step + 1, sign), halves[sign] if step == 0 else (0, 192))
        r[where] = (r[where].astype(F32) + got[...].astype(F32)).astype(BF16)

    for sign in (1, -1):
        ring_send("z", sign, 0)
    links.wait(y_id, ryo, dev_yt)
    r[yb, :, :, lo] = (r[yb, :, :, lo].astype(F32) + ryo[...].astype(F32)).astype(BF16)
    for sign in (1, -1):
        ring_send("y", sign, 0)
    for step in range(1, 4):
        for kind in ("z", "y"):
            for sign in (1, -1):
                ring_add(kind, sign, step - 1)
                ring_send(kind, sign, step)
    got = [ring_recv("z", sign, 3) for sign in (1, -1)]
    total = r[:, zlo, zhi, hi].astype(F32) + got[0][...].astype(F32) + got[1][...].astype(F32)
    fin[...] = total
    fins[...] = total.astype(BF16)
    fin_id = links.ids()
    links.send(fin_id, fins.at[1 - yb], yfin, dev_yt)
    got = [ring_recv("y", sign, 3) for sign in (1, -1)]
    out_ref[lo, :] = (r[yb, zlo, zhi, lo].astype(F32) + got[0][...].astype(F32) + got[1][...].astype(F32)).astype(BF16)
    links.wait(fin_id, yfin, dev_yt)
    out_ref[hi, :] = (fin[yb] + yfin[...].astype(F32)).astype(BF16)

    for own, copy, stay in stage:
        @pl.when(jnp.logical_not(own))
        def _():
            copy.wait_send()
    links.drain()


def on_device(key_rows, value_rows, token_rates, query_rows, fast_gate, fast_up, fast_down):
    any_spec = pl.BlockSpec(memory_space=pl.ANY)
    vmem = pl.BlockSpec(memory_space=pltpu.VMEM)
    V = pltpu.VMEM
    scratch = [
        V((1536, 1024), BF16), V((1536, 1024), BF16), V((1536, 1024), BF16), V((1, 1536), F32),
        V((3, 128, 384), BF16), V((3, 384, 1024), BF16),
        V((384, 1536), F32), V((384, 1536), F32), V((384, 1536), BF16), V((2, 384, 1536), BF16),
        V((3, 4, 2, 48, 1024), BF16),
        V((4, 48, 1024), BF16), V((48, 512), BF16), V((48, 512), BF16), V((48, 1024), BF16), V((48, 1024), BF16),
        V((2, 2, 48, 512), BF16), V((2, 2, 48, 512), BF16), V((2, 2, 48, 1024), BF16), V((2, 2, 48, 1024), BF16),
        V((2, 2, 48, 1024), F32), V((2, 2, 48, 1024), BF16), V((2, 48, 1024), BF16),
        V((3, 4, 2, 48, 1024), BF16),
        V((4, 2, 4, 384, 128), BF16), V((4, 4, 384, 128), BF16), V((2, 2, 4, 384, 128), BF16),
        V((2, 4, 192, 128), BF16),
        V((2, 96, 128), BF16), V((2, 96, 128), BF16), V((3, 2, 192, 128), BF16), V((3, 2, 192, 128), BF16),
        V((96, 128), BF16), V((96, 128), BF16), V((3, 192, 128), BF16), V((3, 192, 128), BF16),
        V((2, 192, 128), F32), V((2, 192, 128), BF16), V((192, 128), BF16),
        pltpu.SemaphoreType.DMA((N_SEM,)), pltpu.SemaphoreType.DMA((N_SEM,)), pltpu.SemaphoreType.DMA((8,)),
    ]
    return pl.pallas_call(
        kernel,
        out_shape=jax.ShapeDtypeStruct((384, 128), BF16),
        in_specs=[any_spec, any_spec, any_spec, any_spec, any_spec, any_spec, any_spec],
        out_specs=vmem,
        scratch_shapes=scratch,
        compiler_params=pltpu.CompilerParams(
            collective_id=0, has_side_effects=True, vmem_limit_bytes=58 * 2**20),
        name="ttt",
    )(key_rows, value_rows, token_rates.reshape(1, 384), query_rows, fast_gate, fast_up, fast_down.T)


def solution(mesh):
    placed = (
        P("ctx", None), P("ctx", None), P("ctx"), P("ctx", None),
        P("ctx", "state"), P("ctx", "state"), P("state", "ctx"),
    )
    return jax.shard_map(
        on_device, mesh=mesh, in_specs=placed, out_specs=P("ctx", "state"), check_vma=False)
```

time: 1230 us -> 122 us (0.10)
  waiting for transfers between devices: 852 us -> 0 us
  blocking collectives: 306 us -> 0 us
  Pallas kernels: 0 us -> 117 us
  matrix products: 30.4 us -> 0 us
  local copies, waits for them, and re-layouts: 18.3 us -> 2.78 us
  between operations: 13.6 us -> 0.01 us
  other arithmetic: 12.5 us -> 0 us
    all_gather x4 -> x0, waiting for transfers between devices: 635 us -> none  [the longest x1 170 us: on_device(): renewed_full = lax.all_gather(renewed, 'ctx', axis=0, tiled=True)]
    psum x2 -> x0, blocking collectives: 306 us -> none  [the longest x1 154 us: on_device(): stepped_sq = lax.psum(jnp.sum(stepped * stepped, axis=0), 'ctx')]
    reduce_scatter x1 -> x0, waiting for transfers between devices: 175 us -> none  [on_device(): lax.psum_scatter(jnp.concatenate([lax.dot_general(key_rows, grad_gate, co...]
    pallas_call x0 -> x1, Pallas kernels: none -> 117 us  [on_device(): pl.pallas_call(kernel, out_shape=jax.ShapeDtypeStruct((384, 128), BF16),...]
    unnamed x7 -> x0, waiting for transfers between devices: 42 us -> none
    dot_general x8 -> x0, matrix products: 30.4 us -> none  [the longest x1 6.19 us: on_device(): lax.dot_general(hidden_next, renewed_full[:, 2 * hidden_width:], contract...]
    unnamed x31 -> x1, local copies, waits for them, and re-layouts: 18.3 us -> 1.54 us
  transfers between devices with their start and end apart: 6 -> 0, of which waited for: 6 -> 0; matrix products, arithmetic and copies ran while one was open for 1% -> 0% of each run, Pallas kernels for 0% -> 0%
where the time goes in v1:
time: 122 us; the launch traced here: 120 us
  Pallas kernels  117 us (96%)
  local copies, waits for them, and re-layouts  2.78 us (2%)
    pallas_call x1, Pallas kernels, on_device(): pl.pallas_call(kernel, out_shape=jax.ShapeDtypeStruct((384, 128), BF16),...  117 us

profile of v1, /device:TPU:8, one launch (start us, length us, event | category | flops | bytes accessed | tf_op | source)
XLA Modules:
  0.0 119.8 jit_solution(6568073852287268973)
XLA Ops:
  0.0 1.2 %reshape.3.rate_ref = f32[1,384]{1,0:T(1,128)} reshape(f32[384]{0:T(512)} %param.9) | data formatting | bytes 3072 | tf_op jit(solution)/shard_map/reshape | solution.py:483
  1.2 117.0 %ttt.1 = bf16[384,128]{1,0:T(8,128)(2,1)} custom-call(bf16[384,1024]{1,0:T(8,128)(2,1)} %key_ref.1, bf16[384,1024]{1,0:T(8,128)(2,1)} %val_ref.1, f32[1,384]{1,0:T(1,128)} %reshape.3.rate_ref, bf16[384,1024]{1,0:T(8,128)(2,1)} %qry_ref.1, bf16[32,1536]{1,0:T(8,128)(2,1)} %gate_ref.1, bf16[32,1536]{1,0:T(8,128)(2,1)} %up_ref.1, bf16[32,1536]{1,0:T(8,128)(2,1)} %bitcast.1), custom_call_target="tpu_custom_call" | custom-call | tf_op jit(solution)/shard_map/ttt/pallas_call | solution.py:474
  118.2 1.5 %copy.9 = bf16[384,128]{1,0:T(8,128)(2,1)} copy(bf16[384,128]{1,0:T(8,128)(2,1)} %ttt.1) | data formatting | bytes 196608

commit v2 on v0

v2 whole, which is shorter than its diff:
```python
import functools

import jax
import jax.numpy as jnp
from jax import lax
from jax.experimental import pallas as pl
from jax.experimental.pallas import tpu as pltpu
from jax.sharding import PartitionSpec as P

MESH = pl.DeviceIdType.MESH
EPS = 1e-06
RATE = 0.5
NT = (((1,), (1,)), ((), ()))
NN = (((1,), (0,)), ((), ()))
F32, BF16 = jnp.float32, jnp.bfloat16
N_SEM = 224


def dot(a, b, dims):
    return lax.dot_general(a, b, dims, preferred_element_type=F32)


def place(x, y, z, k):
    return (x * 8 + (z % 2) * 4 + y, (z // 2) * 2 + k)


class Links:
    def __init__(self, send_sem, recv_sem):
        self.send_sem, self.recv_sem, self.used, self.sent = send_sem, recv_sem, 0, []

    def ids(self, count=1):
        first = self.used
        self.used += count
        assert self.used <= N_SEM
        return first

    def send(self, index, src, dst, device):
        copy = pltpu.make_async_remote_copy(
            src_ref=src, dst_ref=dst, send_sem=self.send_sem.at[index], recv_sem=self.recv_sem.at[index],
            device_id=device, device_id_type=MESH)
        copy.start()
        self.sent.append(copy)

    def wait(self, index, dst, device):
        pltpu.make_async_remote_copy(
            src_ref=dst, dst_ref=dst, send_sem=self.send_sem.at[index], recv_sem=self.recv_sem.at[index],
            device_id=device, device_id_type=MESH).wait_recv()

    def drain(self):
        for copy in self.sent:
            copy.wait_send()


def kernel(key_ref, val_ref, rate_ref, qry_ref, gate_ref, up_ref, down_ref, out_ref,
           key_all, val_all, qry_all, rates, rate_row, raw, w, gp, uq, hid, grads,
           d, ry0, x1a0, x1b0, x2a0, x2b0, x1a, x1b, x2a, x2b, es, ry, new,
           act, ob, osib, r, ryo, slot0, slots, fin, fins, yfin,
           send_sem, recv_sem, local_sem):
    c, s = lax.axis_index("ctx"), lax.axis_index("state")
    x, zlo, y = c // 8, (c // 4) % 2, c % 4
    zhi, k = s // 2, s % 2
    z = 2 * zhi + zlo
    p, yb = y // 2, y % 2
    xp, xm, xo = (x + 1) % 4, (x + 3) % 4, (x + 2) % 4
    zp, zm = (z + 1) % 8, (z + 7) % 8
    yt = y + 1 - 2 * yb
    yr = 3 - y
    po = 1 - p
    y2 = ((y + 1) // 2) % 2
    links = Links(send_sem, recv_sem)
    z_pair = z + 1 - 2 * zlo
    dev_xp, dev_xm = place(xp, y, z, k), place(xm, y, z, k)
    dev_yt, dev_yr = place(x, yt, z, k), place(x, yr, z, k)
    dev_zp, dev_zm = place(x, y, zp, k), place(x, y, zm, k)
    dev_core = place(x, y, z, 1 - k)
    dev_pair, dev_diag = place(x, y, z_pair, k), place(x, yt, z_pair, k)

    barrier = pltpu.get_barrier_semaphore()
    for other in (dev_xp, dev_xm, dev_yt, dev_yr, dev_zp, dev_zm, dev_diag, dev_core):
        pl.semaphore_signal(barrier, inc=1, device_id=other, device_id_type=MESH)

    def block(yy, zz):
        return 2 * yy + zz

    me = block(yb, zlo)

    full = [key_all, val_all, qry_all]
    src = [key_ref, val_ref, qry_ref]
    weights = [gate_ref, up_ref, down_ref]

    def share(a, qz, q2):
        return weights[a].at[:, pl.ds(pl.multiple_of((qz * 2 + q2) * 384, 128), 384)]

    stay = []
    for a in range(3):
        copy = pltpu.make_async_copy(share(a, zlo, y2), raw.at[c, a], local_sem.at[a])
        copy.start()
        stay.append(copy)
    rate_copy = pltpu.make_async_copy(rate_ref, rate_row, local_sem.at[6])
    rate_copy.start()
    local = []
    for i in range(3):
        copy = pltpu.make_async_copy(
            src[i], full[i].at[pl.ds(pl.multiple_of(me * 384, 16), 384)], local_sem.at[3 + i])
        copy.start()
        local.append(copy)
    pl.semaphore_wait(barrier, 8)

    st = {(a, j): links.ids() for a in range(3) for j in (1, 2, 3)}
    for a in range(3):
        links.send(st[a, 3], share(a, 1 - zlo, 1 - y2), raw.at[c, a], dev_diag)
        links.send(st[a, 1], share(a, zlo, 1 - y2), raw.at[c, a], dev_yt)
        links.send(st[a, 2], share(a, 1 - zlo, y2), raw.at[c, a], dev_pair)

    blocks = {"a": block(1 - yb, zlo), "b": block(yb, 1 - zlo), "c": block(1 - yb, 1 - zlo)}
    fine = [[(0, 16), (16, 32), (96, 48), (48, 48), (144, 48)],
            [(0, 48), (96, 48), (48, 32), (144, 32), (80, 16), (176, 16)],
            [(0, 96), (96, 96)]]
    coarse = [(0, 96), (96, 96)]

    def parts(i, kind):
        return coarse if kind == "b" else fine[i]

    tok_ids = {(i, kind, h): links.ids() for i in range(3) for kind in "abc" for h in parts(i, kind)}
    sib_ids = {(i, kind, h): links.ids() for i in range(3) for kind in "abc" for h in parts(i, kind)}

    def rows(i, b, h, kk=k):
        return full[i].at[pl.ds(pl.multiple_of(b * 384 + kk * 192 + h[0], 16), h[1])]

    z_to = [dev_zp, dev_zm]

    def a_start(i, h):
        mine = src[i].at[pl.ds(pl.multiple_of(k * 192 + h[0], 16), h[1])]
        links.send(tok_ids[i, "a", h], mine, rows(i, me, h), dev_yt)

    def b_start(i):
        for h in coarse:
            mine = src[i].at[pl.ds(pl.multiple_of(k * 192 + h[0], 16), h[1])]
            links.send(tok_ids[i, "b", h], mine, rows(i, me, h), z_to[h[0] // 96])

    def token_pass(i, kind, hs=None):
        for h in hs or parts(i, kind):
            here = rows(i, blocks[kind], h)
            links.wait(tok_ids[i, kind, h], here, dev_core)
            if kind == "a":
                links.send(tok_ids[i, "c", h], here, here, z_to[h[0] // 96])
            links.send(sib_ids[i, kind, h], here, here, dev_core)

    queue = [(i, h) for i in range(2) for h in fine[i]]

    def a_pass(n, ahead=3):
        i, h = queue[n]
        here = rows(i, blocks["a"], h)
        links.wait(tok_ids[i, "a", h], here, dev_core)
        if n + ahead < len(queue):
            a_start(*queue[n + ahead])
        links.send(tok_ids[i, "c", h], here, here, z_to[h[0] // 96])
        links.send(sib_ids[i, "a", h], here, here, dev_core)

    def token_finish(i, kinds="abc"):
        for kind in kinds:
            for h in parts(i, kind):
                links.wait(sib_ids[i, kind, h], rows(i, blocks[kind], h, 1 - k), dev_core)

    def gather(late, piece, half):
        ids = {}

        def at(name, j):
            if (name, j) not in ids:
                ids[name, j] = links.ids()
            return ids[name, j]

        def move(name, j, ref, device):
            links.send(at(name, j), ref, ref, device)

        def start(j, along_y=True):
            if along_y:
                move("y", j, piece(j, x, 0), dev_yr)
            move("xp", j, piece(j, x, 0), dev_xp)
            move("xm", j, piece(j, x, 0), dev_xm)

        def start_y(j):
            move("y", j, piece(j, x, 0), dev_yr)

        def cross(j):
            links.wait(at("y", j), piece(j, x, 1), dev_yr)
            move("xp2", j, piece(j, x, 1), dev_xp)
            move("xm2", j, piece(j, x, 1), dev_xm)

        def onward(j, other=0):
            which = "2" if other else ""
            links.wait(at("xp" + which, j), piece(j, xm, other), dev_xm)
            move("fp" + which, j, half(j, xm, other, 0), dev_xp)
            if j in late:
                move("y1", j, piece(j, xm, 0), dev_yr)
            links.wait(at("xm" + which, j), piece(j, xp, other), dev_xp)
            move("fm" + which, j, half(j, xp, other, 1), dev_xm)
            if j in late:
                move("y2", j, piece(j, xp, 0), dev_yr)

        def far(j, other=0):
            which = "2" if other else ""
            links.wait(at("fp" + which, j), half(j, xo, other, 0), dev_xm)
            links.wait(at("fm" + which, j), half(j, xo, other, 1), dev_xp)
            if j in late:
                move("y3", j, piece(j, xo, 0), dev_yr)

        def finish(j):
            if j in late:
                links.wait(at("y", j), piece(j, x, 1), dev_yr)
                links.wait(at("y1", j), piece(j, xm, 1), dev_yr)
                links.wait(at("y2", j), piece(j, xp, 1), dev_yr)
                links.wait(at("y3", j), piece(j, xo, 1), dev_yr)
            else:
                far(j, 1)

        return start, start_y, cross, onward, far, finish

    def source(j, xx, other):
        yy = yt if j % 2 else y
        return xx * 8 + (1 - zlo if j >= 2 else zlo) * 4 + (3 - yy if other else yy)

    def w_piece(j, xx, other):
        return raw.at[source(j, xx, other)]

    def w_half(j, xx, other, h):
        return raw.at[source(j, xx, other), :, pl.ds(16 * h, 16)]

    w_start, w_start_y, w_cross, w_onward, w_far, w_finish = gather((2,), w_piece, w_half)
    for copy in stay:
        copy.wait()
    w_start(0)
    for n in range(3):
        a_start(*queue[n])
    b_start(0)
    rate_copy.wait()
    rate_id = links.ids(3)

    def rate_at(b):
        return rates.at[:, pl.ds(pl.multiple_of(b * 384, 128), 384)]

    rate_at(me)[...] = rate_row[...].reshape(1, 384)
    links.send(rate_id, rate_at(me), rate_at(me), dev_yt)
    links.send(rate_id + 1, rate_at(me), rate_at(me), dev_pair)
    links.send(rate_id + 2, rate_at(me), rate_at(me), dev_diag)

    def w_arrived(j):
        for a in range(3):
            links.wait(st[a, j], raw.at[source(j, x, 0), a], dev_core)
        w_start(j, j != 2)

    w_onward(0)
    w_cross(0)
    w_arrived(1)
    w_arrived(3)
    w_arrived(2)
    a_pass(0)
    w_onward(0, 1)
    a_pass(1)
    a_pass(2)
    w_cross(1)
    w_cross(3)
    w_start_y(2)
    a_pass(3)
    token_pass(0, "b")
    b_start(1)
    w_onward(2)
    w_onward(1)
    w_onward(3)
    a_pass(4)
    w_onward(1, 1)
    a_pass(5)
    a_pass(6)
    w_far(2)
    a_pass(7)
    w_onward(3, 1)
    token_pass(0, "c")
    token_pass(1, "b")
    a_pass(8)
    for copy in local:
        copy.wait()
    for i, b in enumerate(("a", "b", "c")):
        links.wait(rate_id + i, rate_at(blocks[b]), dev_core)

    def upright(zz):
        for a in range(3):
            for xx in range(4):
                g = 2 * xx + zz
                w[a, :, pl.ds(pl.multiple_of(128 * g, 128), 128)] = (
                    raw[pl.ds(4 * g, 4), a].reshape(128, 384).astype(F32).T.astype(BF16))

    for j in (0, 1):
        w_far(j)
        w_finish(j)
    upright(zlo)
    a_pass(9)
    w_far(3)
    w_finish(3)
    a_pass(10)
    w_finish(2)
    upright(1 - zlo)

    def forward(yy):
        cols = pl.ds(pl.multiple_of(yy * 768, 256), 768)
        keys = key_all[cols, :]
        gate_pre = dot(w[0], keys, NT)
        up_pre = dot(w[1], keys, NT)
        gp[:, cols] = gate_pre
        uq[:, cols] = up_pre
        hid[:, cols] = (gate_pre * jax.nn.sigmoid(gate_pre) * up_pre * rates[:, cols]).astype(BF16)

    def backward(yy):
        cols = pl.ds(pl.multiple_of(yy * 768, 256), 768)
        back = dot(w[2], val_all[cols, :], NT) * rates[:, cols]
        gate_pre, up_pre = gp[:, cols], uq[:, cols]
        sig = jax.nn.sigmoid(gate_pre)
        grads[0, :, cols] = (back * up_pre * sig * (1.0 + gate_pre * (1.0 - sig))).astype(BF16)
        grads[1, :, cols] = (back * gate_pre * sig).astype(BF16)

    token_finish(0, "b")
    forward(yb)
    token_pass(1, "c")
    token_finish(0, "ac")
    forward(1 - yb)
    token_finish(1, "b")
    backward(yb)
    token_finish(1, "ac")
    for h in fine[2]:
        a_start(2, h)
    b_start(2)

    def direction(a, acts, tokens):
        d[a] = dot(acts[...], tokens[...], NN).reshape(4, 2, 48, 1024).astype(BF16)

    rs = {name: links.ids(3) for name in ("ap", "bm", "p", "m", "p2", "m2", "y")}
    ab = [pl.ds(0, 512), pl.ds(512, 512)]

    def reduce_start(a):
        links.send(rs["ap"] + a, d.at[a, xo, :, :, ab[0]], x1a.at[a - 1], dev_xp)
        links.send(rs["bm"] + a, d.at[a, xo, :, :, ab[1]], x1b.at[a - 1], dev_xm)

    def reduce_merge(a):
        links.wait(rs["ap"] + a, x1a.at[a - 1], dev_xm)
        d[a, xp, :, :, ab[0]] = d[a, xp, :, :, ab[0]] + x1a[a - 1]
        links.send(rs["p"] + a, d.at[a, xp, po], x2a.at[a - 1, po], dev_xp)
        links.wait(rs["bm"] + a, x1b.at[a - 1], dev_xp)
        d[a, xm, :, :, ab[1]] = d[a, xm, :, :, ab[1]] + x1b[a - 1]
        links.send(rs["m"] + a, d.at[a, xm, po], x2b.at[a - 1, po], dev_xm)

    def reduce_own(a):
        links.send(rs["p2"] + a, d.at[a, xp, p], x2a.at[a - 1, p], dev_xp)
        links.send(rs["m2"] + a, d.at[a, xm, p], x2b.at[a - 1, p], dev_xm)

    def row_total(a, pp):
        return d[a, x, pp].astype(F32) + x2a[a - 1, pp].astype(F32) + x2b[a - 1, pp].astype(F32)

    def reduce_cross(a):
        links.wait(rs["p"] + a, x2a.at[a - 1, po], dev_xm)
        links.wait(rs["m"] + a, x2b.at[a - 1, po], dev_xp)
        es[a - 1] = row_total(a, po).astype(BF16)
        links.send(rs["y"] + a, es.at[a - 1], ry.at[a - 1], dev_yr)

    def reduce_finish(a):
        links.wait(rs["p2"] + a, x2a.at[a - 1, p], dev_xm)
        links.wait(rs["m2"] + a, x2b.at[a - 1, p], dev_xp)
        links.wait(rs["y"] + a, ry.at[a - 1], dev_yr)
        renew(a, row_total(a, p) + ry[a - 1].astype(F32))

    def renew(a, grad):
        unit = pl.ds(pl.multiple_of((2 * x + p) * 48, 16), 48)
        old = w[a, unit, :].astype(F32)
        norm = jnp.sqrt(jnp.sum(old * old, axis=1, keepdims=True) + EPS)
        stepped = old + RATE * norm / jnp.sqrt(jnp.sum(grad * grad, axis=1, keepdims=True) + EPS) * grad
        scale = norm / jnp.sqrt(jnp.sum(stepped * stepped, axis=1, keepdims=True) + EPS)
        new[a, x, p] = (stepped * scale).astype(BF16)

    direction(2, hid, val_all)
    reduce_start(2)
    backward(1 - yb)
    direction(0, grads.at[0], key_all)
    cross_ids = links.ids(5)

    def cross_ref(n, ref, lead):
        if n < 2:
            return ref.at[lead + (xo,) + ((po,) if lead else ()) + (slice(None), ab[n])]
        return ref.at[lead + ((xp, xm, x)[n - 2],) + ((po,) if lead else ())]

    def cross_send(n):
        links.send(cross_ids + n, cross_ref(n, d, (0,)), cross_ref(n, ry0, ()), dev_yr)

    def cross_add(n):
        links.wait(cross_ids + n, cross_ref(n, ry0, ()), dev_yr)
        if n < 2:
            d[0, xo, p, :, ab[n]] = d[0, xo, p, :, ab[n]] + ry0[xo, :, ab[n]]
        else:
            to_x = (xp, xm, x)[n - 2]
            d[0, to_x, p] = d[0, to_x, p] + ry0[to_x]

    cross_send(0)
    cross_send(1)
    direction(1, grads.at[1], key_all)
    reduce_merge(2)
    reduce_start(1)
    cross_send(2)
    cross_send(3)
    token_pass(2, "b")
    cross_add(0)
    links.send(rs["ap"], d.at[0, xo, p, :, ab[0]], x1a0, dev_xp)
    cross_add(1)
    links.send(rs["bm"], d.at[0, xo, p, :, ab[1]], x1b0, dev_xm)
    reduce_own(2)
    reduce_cross(2)
    cross_send(4)
    reduce_merge(1)
    cross_add(2)
    links.wait(rs["ap"], x1a0, dev_xm)
    d[0, xp, p, :, ab[0]] = d[0, xp, p, :, ab[0]] + x1a0[...]
    links.send(rs["p"], d.at[0, xp, p], x2a0, dev_xp)
    cross_add(3)
    links.wait(rs["bm"], x1b0, dev_xp)
    d[0, xm, p, :, ab[1]] = d[0, xm, p, :, ab[1]] + x1b0[...]
    links.send(rs["m"], d.at[0, xm, p], x2b0, dev_xm)
    reduce_own(1)
    token_pass(2, "a")

    def n_piece(a, xx, other):
        return new.at[a, xx, po if other else p]

    def n_half(a, xx, other, h):
        return new.at[a, xx, po if other else p, :, ab[h]]

    n_start, n_start_y, n_cross, n_onward, n_far, n_finish = gather((1,), n_piece, n_half)
    reduce_cross(1)
    reduce_finish(2)
    n_start(2)
    cross_add(4)
    links.wait(rs["p"], x2a0, dev_xm)
    links.wait(rs["m"], x2b0, dev_xp)
    renew(0, d[0, x, p].astype(F32) + x2a0[...].astype(F32) + x2b0[...].astype(F32))
    n_start(0)
    reduce_finish(1)
    n_start(1)
    token_pass(2, "c")
    n_onward(2)
    n_cross(2)
    n_onward(0)
    n_cross(0)
    n_onward(1)
    n_onward(2, 1)
    n_onward(0, 1)
    n_far(1)
    token_finish(2)
    n_far(2)
    n_far(0)
    n_finish(2)
    n_finish(0)

    core_ids = links.ids(4)
    y_ids = {(i, j): links.ids() for i in range(2) for j in range(4)}
    lo, hi = pl.ds(0, 192), pl.ds(192, 192)

    def queries(i):
        b = block(yb if i % 2 else 1 - yb, zlo if i < 2 else 1 - zlo)
        return qry_all[pl.ds(pl.multiple_of(b * 384, 16), 384), :]

    def gate(i):
        gate_next = dot(queries(i), new[0].reshape(384, 1024), NT)
        act[i] = gate_next * jax.nn.sigmoid(gate_next)

    def apply(i):
        up_next = dot(queries(i), new[1].reshape(384, 1024), NT)
        term = dot((act[i] * up_next).astype(BF16), new[2].reshape(384, 1024), NN)
        for zz in range(4):
            for kk in range(2):
                at = (2 * zz + kk) * 128
                ob[i, kk, zz] = term[:, at:at + 128].astype(BF16)
        links.send(core_ids + i, ob.at[i, 1 - k], osib.at[i], dev_core)

    def both_cores(i):
        links.wait(core_ids + i, osib.at[i], dev_core)
        r[i // 2, i % 2] = ob[i, k] + osib[i]

    streams = ("far", "own", "y")
    ring = {(kind, sign): links.ids(4) for kind in streams for sign in (1, -1)}

    def to(step, sign):
        return ((z + sign * (4 - step) + 8) % 8) // 2

    targets = [(to(0, 1), to(2, 1), to(2, -1), zhi), (to(1, 1), to(1, -1), to(3, 1), to(3, -1))]

    def y_send(i, js):
        for j in js:
            t = targets[i][j]
            links.send(y_ids[i, j], r.at[i, 0, t, lo], ryo.at[i, t], dev_yt)

    def y_add(i, js):
        for j in js:
            t = targets[i][j]
            links.wait(y_ids[i, j], ryo.at[i, t], dev_yt)
            r[i, 1, t, lo] = r[i, 1, t, lo] + ryo[i, t]

    def chunk(kind, step, sign, part):
        base = 0 if kind == "y" else 192
        return (step % 2, 0 if kind == "far" else 1, to(step, sign), pl.ds(base + part[0], part[1]))

    halves = {1: (0, 96), -1: (96, 96)}

    def slot(kind, sign, step):
        n = 2 * streams.index(kind) + (0 if sign > 0 else 1)
        return slot0.at[n] if step == 0 else slots.at[n, step - 1]

    def ring_send(kind, sign, step):
        part = halves[sign] if step == 0 else (0, 192)
        links.send(ring[kind, sign] + step, r.at[chunk(kind, step, sign, part)],
                   slot(kind, sign, step), dev_zp if sign > 0 else dev_zm)

    def ring_recv(kind, sign, step):
        got = slot(kind, sign, step)
        links.wait(ring[kind, sign] + step, got, dev_zm if sign > 0 else dev_zp)
        return got

    def ring_add(kind, sign, step):
        got = ring_recv(kind, sign, step)
        where = chunk(kind, step + 1, sign, halves[sign] if step == 0 else (0, 192))
        r[where] = r[where] + got[...]

    def ring_step(kind, step):
        for sign in (1, -1):
            if step:
                ring_add(kind, sign, step - 1)
            ring_send(kind, sign, step)

    def ring_total(kind, i, rows_at):
        got = [ring_recv(kind, sign, 3)[...].astype(F32) for sign in (1, -1)]
        return r[0, i, zhi, rows_at].astype(F32) + got[0] + got[1]

    for i in range(4):
        gate(i)
    n_finish(1)
    apply(0)
    apply(2)
    both_cores(0)
    y_send(0, (0,))
    ring_step("far", 0)
    apply(1)
    both_cores(2)
    y_send(1, (0, 1))
    y_send(0, (1, 2))
    apply(3)
    both_cores(1)
    ring_step("own", 0)
    y_add(0, (0,))
    ring_step("y", 0)
    y_send(1, (2, 3))
    y_send(0, (3,))
    ring_step("far", 1)
    both_cores(3)
    ring_step("own", 1)
    y_add(1, (0, 1))
    ring_step("y", 1)
    ring_step("far", 2)
    ring_step("own", 2)
    y_add(0, (1, 2))
    ring_step("y", 2)
    ring_step("far", 3)
    ring_step("own", 3)
    y_add(1, (2, 3))
    ring_step("y", 3)
    y_add(0, (3,))
    fins[...] = ring_total("far", 0, hi).astype(BF16)
    fin_id = links.ids()
    links.send(fin_id, fins, yfin, dev_yt)
    fin[...] = ring_total("own", 1, hi)
    out_ref[lo, :] = ring_total("y", 1, lo).astype(BF16)
    links.wait(fin_id, yfin, dev_yt)
    out_ref[hi, :] = (fin[...] + yfin[...].astype(F32)).astype(BF16)
    links.drain()


def on_device(key_rows, value_rows, token_rates, query_rows, fast_gate, fast_up, fast_down):
    any_spec = pl.BlockSpec(memory_space=pl.ANY)
    vmem = pl.BlockSpec(memory_space=pltpu.VMEM)
    V = pltpu.VMEM
    scratch = [
        V((1536, 1024), BF16), V((1536, 1024), BF16), V((1536, 1024), BF16), V((1, 1536), F32),
        V((384,), F32), V((32, 3, 32, 384), BF16), V((3, 384, 1024), BF16),
        V((384, 1536), F32), V((384, 1536), F32), V((384, 1536), BF16), V((2, 384, 1536), BF16),
        V((3, 4, 2, 48, 1024), BF16),
        V((4, 48, 1024), BF16), V((48, 512), BF16), V((48, 512), BF16), V((48, 1024), BF16), V((48, 1024), BF16),
        V((2, 2, 48, 512), BF16), V((2, 2, 48, 512), BF16), V((2, 2, 48, 1024), BF16), V((2, 2, 48, 1024), BF16),
        V((2, 48, 1024), BF16), V((2, 48, 1024), BF16),
        V((3, 4, 2, 48, 1024), BF16),
        V((4, 384, 384), F32), V((4, 2, 4, 384, 128), BF16), V((4, 4, 384, 128), BF16), V((2, 2, 4, 384, 128), BF16),
        V((2, 4, 192, 128), BF16),
        V((6, 96, 128), BF16), V((6, 3, 192, 128), BF16),
        V((192, 128), F32), V((192, 128), BF16), V((192, 128), BF16),
        pltpu.SemaphoreType.DMA((N_SEM,)), pltpu.SemaphoreType.DMA((N_SEM,)), pltpu.SemaphoreType.DMA((8,)),
    ]
    return pl.pallas_call(
        kernel,
        out_shape=jax.ShapeDtypeStruct((384, 128), BF16),
        in_specs=[any_spec, any_spec, any_spec, any_spec, any_spec, any_spec, any_spec],
        out_specs=vmem,
        scratch_shapes=scratch,
        compiler_params=pltpu.CompilerParams(
            collective_id=0, has_side_effects=True, vmem_limit_bytes=58 * 2**20),
        name="ttt",
    )(key_rows, value_rows, token_rates, query_rows, fast_gate, fast_up, fast_down.T)


def solution(mesh):
    placed = (
        P("ctx", None), P("ctx", None), P("ctx"), P("ctx", None),
        P("ctx", "state"), P("ctx", "state"), P("state", "ctx"),
    )
    return jax.shard_map(
        on_device, mesh=mesh, in_specs=placed, out_specs=P("ctx", "state"), check_vma=False)
```

time: 1230 us -> 103 us (0.08)
  waiting for transfers between devices: 852 us -> 0 us
  blocking collectives: 306 us -> 0 us
  Pallas kernels: 0 us -> 102 us
  matrix products: 30.4 us -> 0 us
  local copies, waits for them, and re-layouts: 18.3 us -> 1.54 us
  between operations: 13.6 us -> 0.01 us
  other arithmetic: 12.5 us -> 0 us
    all_gather x4 -> x0, waiting for transfers between devices: 635 us -> none  [the longest x1 170 us: on_device(): renewed_full = lax.all_gather(renewed, 'ctx', axis=0, tiled=True)]
    psum x2 -> x0, blocking collectives: 306 us -> none  [the longest x1 154 us: on_device(): stepped_sq = lax.psum(jnp.sum(stepped * stepped, axis=0), 'ctx')]
    reduce_scatter x1 -> x0, waiting for transfers between devices: 175 us -> none  [on_device(): lax.psum_scatter(jnp.concatenate([lax.dot_general(key_rows, grad_gate, co...]
    pallas_call x0 -> x1, Pallas kernels: none -> 102 us  [on_device(): pl.pallas_call(kernel, out_shape=jax.ShapeDtypeStruct((384, 128), BF16),...]
    unnamed x7 -> x0, waiting for transfers between devices: 42 us -> none
    dot_general x8 -> x0, matrix products: 30.4 us -> none  [the longest x1 6.19 us: on_device(): lax.dot_general(hidden_next, renewed_full[:, 2 * hidden_width:], contract...]
    unnamed x31 -> x1, local copies, waits for them, and re-layouts: 18.3 us -> 1.54 us
  transfers between devices with their start and end apart: 6 -> 0, of which waited for: 6 -> 0; matrix products, arithmetic and copies ran while one was open for 1% -> 0% of each run, Pallas kernels for 0% -> 0%
where the time goes in v2:
time: 103 us
  Pallas kernels  102 us (99%)
  local copies, waits for them, and re-layouts  1.54 us (1%)
    pallas_call x1, Pallas kernels, on_device(): pl.pallas_call(kernel, out_shape=jax.ShapeDtypeStruct((384, 128), BF16),...  102 us

profile of v2, /device:TPU:8, one launch (start us, length us, event | category | flops | bytes accessed | tf_op | source)
XLA Modules:
  0.0 103.3 jit_solution(12986045344121050407)
XLA Ops:
  0.0 101.7 %ttt.1 = bf16[384,128]{1,0:T(8,128)(2,1)} custom-call(bf16[384,1024]{1,0:T(8,128)(2,1)} %key_ref.1, bf16[384,1024]{1,0:T(8,128)(2,1)} %val_ref.1, f32[384]{0:T(512)} %rate_ref.1, bf16[384,1024]{1,0:T(8,128)(2,1)} %qry_ref.1, bf16[32,1536]{1,0:T(8,128)(2,1)} %gate_ref.1, bf16[32,1536]{1,0:T(8,128)(2,1)} %up_ref.1, bf16[32,1536]{1,0:T(8,128)(2,1)} %bitcast.1), custom_call_target="tpu_custom_call" | custom-call | tf_op jit(solution)/shard_map/ttt/pallas_call | solution.py:599
  101.7 1.5 %copy.9 = bf16[384,128]{1,0:T(8,128)(2,1)} copy(bf16[384,128]{1,0:T(8,128)(2,1)} %ttt.1) | data formatting | bytes 196608

commit v3 on v2

--- a/solution.py
+++ b/solution.py
@@ -13,7 +13,7 @@
 NT = (((1,), (1,)), ((), ()))
 NN = (((1,), (0,)), ((), ()))
 F32, BF16 = jnp.float32, jnp.bfloat16
-N_SEM = 224
+N_SEND, N_RECV = 48, 171
 
 
 def dot(a, b, dims):
@@ -26,35 +26,41 @@
 
 class Links:
     def __init__(self, send_sem, recv_sem):
-        self.send_sem, self.recv_sem, self.used, self.sent = send_sem, recv_sem, 0, []
+        self.send_sem, self.recv_sem, self.used, self.sent, self.turn = send_sem, recv_sem, 0, [], 0
 
     def ids(self, count=1):
         first = self.used
         self.used += count
-        assert self.used <= N_SEM
+        assert self.used <= N_RECV
         return first
 
+    def copy(self, index, src, dst, device, turn=0):
+        return pltpu.make_async_remote_copy(
+            src_ref=src, dst_ref=dst, send_sem=self.send_sem.at[turn], recv_sem=self.recv_sem.at[index],
+            device_id=device, device_id_type=MESH)
+
     def send(self, index, src, dst, device):
-        copy = pltpu.make_async_remote_copy(
-            src_ref=src, dst_ref=dst, send_sem=self.send_sem.at[index], recv_sem=self.recv_sem.at[index],
-            device_id=device, device_id_type=MESH)
+        if len(self.sent) == N_SEND:
+            self.drain(1)
+        copy = self.copy(index, src, dst, device, self.turn % N_SEND)
+        self.turn += 1
         copy.start()
         self.sent.append(copy)
 
     def wait(self, index, dst, device):
-        pltpu.make_async_remote_copy(
-            src_ref=dst, dst_ref=dst, send_sem=self.send_sem.at[index], recv_sem=self.recv_sem.at[index],
-            device_id=device, device_id_type=MESH).wait_recv()
-
-    def drain(self):
-        for copy in self.sent:
+        self.copy(index, dst, dst, device).wait_recv()
+
+    def drain(self, most=300, keep=0):
+        count = max(0, min(most, len(self.sent) - keep))
+        for copy in self.sent[:count]:
             copy.wait_send()
+        del self.sent[:count]
 
 
 def kernel(key_ref, val_ref, rate_ref, qry_ref, gate_ref, up_ref, down_ref, out_ref,
            key_all, val_all, qry_all, rates, rate_row, raw, w, gp, uq, hid, grads,
            d, ry0, x1a0, x1b0, x2a0, x2b0, x1a, x1b, x2a, x2b, es, ry, new,
-           act, ob, osib, r, ryo, slot0, slots, fin, fins, yfin,
+           silu, act, ob, osib, r, ryo, slot0, slots, fin, yfin,
            send_sem, recv_sem, local_sem):
     c, s = lax.axis_index("ctx"), lax.axis_index("state")
     x, zlo, y = c // 8, (c // 4) % 2, c % 4
@@ -74,9 +80,10 @@
     dev_zp, dev_zm = place(x, y, zp, k), place(x, y, zm, k)
     dev_core = place(x, y, z, 1 - k)
     dev_pair, dev_diag = place(x, y, z_pair, k), place(x, yt, z_pair, k)
+    dev_yt_zp, dev_yt_zm = place(x, yt, zp, k), place(x, yt, zm, k)
 
     barrier = pltpu.get_barrier_semaphore()
-    for other in (dev_xp, dev_xm, dev_yt, dev_yr, dev_zp, dev_zm, dev_diag, dev_core):
+    for other in (dev_xp, dev_xm, dev_yt, dev_yr, dev_zp, dev_zm, dev_yt_zp, dev_yt_zm, dev_core):
         pl.semaphore_signal(barrier, inc=1, device_id=other, device_id_type=MESH)
 
     def block(yy, zz):
@@ -104,13 +111,14 @@
             src[i], full[i].at[pl.ds(pl.multiple_of(me * 384, 16), 384)], local_sem.at[3 + i])
         copy.start()
         local.append(copy)
-    pl.semaphore_wait(barrier, 8)
-
-    st = {(a, j): links.ids() for a in range(3) for j in (1, 2, 3)}
+    pl.semaphore_wait(barrier, 9)
+
+    st = {j: links.ids() for j in (1, 2, 3)}
     for a in range(3):
-        links.send(st[a, 3], share(a, 1 - zlo, 1 - y2), raw.at[c, a], dev_diag)
-        links.send(st[a, 1], share(a, zlo, 1 - y2), raw.at[c, a], dev_yt)
-        links.send(st[a, 2], share(a, 1 - zlo, y2), raw.at[c, a], dev_pair)
+        links.send(st[3], share(a, 1 - zlo, 1 - y2), raw.at[c, a], dev_diag)
+        links.send(st[2], share(a, 1 - zlo, y2), raw.at[c, a], dev_pair)
+    for a in range(3):
+        links.send(st[1], share(a, zlo, 1 - y2), raw.at[c, a], dev_yt)
 
     blocks = {"a": block(1 - yb, zlo), "b": block(yb, 1 - zlo), "c": block(1 - yb, 1 - zlo)}
     fine = [[(0, 16), (16, 32), (96, 48), (48, 48), (144, 48)],
@@ -122,7 +130,7 @@
         return coarse if kind == "b" else fine[i]
 
     tok_ids = {(i, kind, h): links.ids() for i in range(3) for kind in "abc" for h in parts(i, kind)}
-    sib_ids = {(i, kind, h): links.ids() for i in range(3) for kind in "abc" for h in parts(i, kind)}
+    sib_ids = {(i, kind): links.ids() for i in range(3) for kind in "abc"}
 
     def rows(i, b, h, kk=k):
         return full[i].at[pl.ds(pl.multiple_of(b * 384 + kk * 192 + h[0], 16), h[1])]
@@ -144,7 +152,7 @@
             links.wait(tok_ids[i, kind, h], here, dev_core)
             if kind == "a":
                 links.send(tok_ids[i, "c", h], here, here, z_to[h[0] // 96])
-            links.send(sib_ids[i, kind, h], here, here, dev_core)
+            links.send(sib_ids[i, kind], here, here, dev_core)
 
     queue = [(i, h) for i in range(2) for h in fine[i]]
 
@@ -155,12 +163,11 @@
         if n + ahead < len(queue):
             a_start(*queue[n + ahead])
         links.send(tok_ids[i, "c", h], here, here, z_to[h[0] // 96])
-        links.send(sib_ids[i, "a", h], here, here, dev_core)
+        links.send(sib_ids[i, "a"], here, here, dev_core)
 
     def token_finish(i, kinds="abc"):
         for kind in kinds:
-            for h in parts(i, kind):
-                links.wait(sib_ids[i, kind, h], rows(i, blocks[kind], h, 1 - k), dev_core)
+            links.wait(sib_ids[i, kind], rows(i, blocks[kind], (0, 192), 1 - k), dev_core)
 
     def gather(late, piece, half):
         ids = {}
@@ -245,8 +252,7 @@
     links.send(rate_id + 2, rate_at(me), rate_at(me), dev_diag)
 
     def w_arrived(j):
-        for a in range(3):
-            links.wait(st[a, j], raw.at[source(j, x, 0), a], dev_core)
+        links.wait(st[j], raw.at[source(j, x, 0)], dev_core)
         w_start(j, j != 2)
 
     w_onward(0)
@@ -269,14 +275,14 @@
     w_onward(3)
     a_pass(4)
     w_onward(1, 1)
+    w_onward(3, 1)
+    w_far(2)
     a_pass(5)
     a_pass(6)
-    w_far(2)
+    token_pass(0, "c", fine[0][:2])
     a_pass(7)
-    w_onward(3, 1)
-    token_pass(0, "c")
+    token_pass(0, "c", fine[0][2:])
     token_pass(1, "b")
-    a_pass(8)
     for copy in local:
         copy.wait()
     for i, b in enumerate(("a", "b", "c")):
@@ -293,12 +299,13 @@
         w_far(j)
         w_finish(j)
     upright(zlo)
-    a_pass(9)
     w_far(3)
     w_finish(3)
+    w_finish(2)
+    a_pass(8)
+    upright(1 - zlo)
+    a_pass(9)
     a_pass(10)
-    w_finish(2)
-    upright(1 - zlo)
 
     def forward(yy):
         cols = pl.ds(pl.multiple_of(yy * 768, 256), 768)
@@ -319,9 +326,10 @@
 
     token_finish(0, "b")
     forward(yb)
-    token_pass(1, "c")
+    token_pass(1, "c", fine[1][:3])
     token_finish(0, "ac")
     forward(1 - yb)
+    token_pass(1, "c", fine[1][3:])
     token_finish(1, "b")
     backward(yb)
     token_finish(1, "ac")
@@ -377,7 +385,8 @@
     direction(2, hid, val_all)
     reduce_start(2)
     backward(1 - yb)
-    direction(0, grads.at[0], key_all)
+    direction(1, grads.at[1], key_all)
+    reduce_start(1)
     cross_ids = links.ids(5)
 
     def cross_ref(n, ref, lead):
@@ -396,14 +405,14 @@
             to_x = (xp, xm, x)[n - 2]
             d[0, to_x, p] = d[0, to_x, p] + ry0[to_x]
 
+    direction(0, grads.at[0], key_all)
     cross_send(0)
     cross_send(1)
-    direction(1, grads.at[1], key_all)
+    cross_send(2)
     reduce_merge(2)
-    reduce_start(1)
-    cross_send(2)
     cross_send(3)
-    token_pass(2, "b")
+    links.drain(40, 25)
+    reduce_merge(1)
     cross_add(0)
     links.send(rs["ap"], d.at[0, xo, p, :, ab[0]], x1a0, dev_xp)
     cross_add(1)
@@ -411,8 +420,10 @@
     reduce_own(2)
     reduce_cross(2)
     cross_send(4)
-    reduce_merge(1)
+    links.drain(25, 25)
     cross_add(2)
+    links.drain(25, 25)
+    reduce_cross(1)
     links.wait(rs["ap"], x1a0, dev_xm)
     d[0, xp, p, :, ab[0]] = d[0, xp, p, :, ab[0]] + x1a0[...]
     links.send(rs["p"], d.at[0, xp, p], x2a0, dev_xp)
@@ -421,6 +432,7 @@
     d[0, xm, p, :, ab[1]] = d[0, xm, p, :, ab[1]] + x1b0[...]
     links.send(rs["m"], d.at[0, xm, p], x2b0, dev_xm)
     reduce_own(1)
+    token_pass(2, "b")
     token_pass(2, "a")
 
     def n_piece(a, xx, other):
@@ -429,31 +441,32 @@
     def n_half(a, xx, other, h):
         return new.at[a, xx, po if other else p, :, ab[h]]
 
-    n_start, n_start_y, n_cross, n_onward, n_far, n_finish = gather((1,), n_piece, n_half)
-    reduce_cross(1)
+    n_start, n_start_y, n_cross, n_onward, n_far, n_finish = gather((0,), n_piece, n_half)
+    links.drain(25, 25)
     reduce_finish(2)
     n_start(2)
+    links.drain(25, 25)
     cross_add(4)
     links.wait(rs["p"], x2a0, dev_xm)
     links.wait(rs["m"], x2b0, dev_xp)
     renew(0, d[0, x, p].astype(F32) + x2a0[...].astype(F32) + x2b0[...].astype(F32))
     n_start(0)
+    links.drain(25, 25)
     reduce_finish(1)
     n_start(1)
     token_pass(2, "c")
+    links.drain(25, 25)
     n_onward(2)
+    links.drain(25, 20)
+    n_onward(0)
+    n_cross(1)
+    n_onward(1)
     n_cross(2)
-    n_onward(0)
-    n_cross(0)
-    n_onward(1)
-    n_onward(2, 1)
-    n_onward(0, 1)
-    n_far(1)
+    links.drain(25, 15)
+    n_far(0)
+    links.drain(25, 12)
+    n_onward(1, 1)
     token_finish(2)
-    n_far(2)
-    n_far(0)
-    n_finish(2)
-    n_finish(0)
 
     core_ids = links.ids(4)
     y_ids = {(i, j): links.ids() for i in range(2) for j in range(4)}
@@ -465,11 +478,13 @@
 
     def gate(i):
         gate_next = dot(queries(i), new[0].reshape(384, 1024), NT)
-        act[i] = gate_next * jax.nn.sigmoid(gate_next)
+        silu[i] = gate_next * jax.nn.sigmoid(gate_next)
+
+    def activate(i):
+        act[i] = (silu[i] * dot(queries(i), new[1].reshape(384, 1024), NT)).astype(BF16)
 
     def apply(i):
-        up_next = dot(queries(i), new[1].reshape(384, 1024), NT)
-        term = dot((act[i] * up_next).astype(BF16), new[2].reshape(384, 1024), NN)
+        term = dot(act[i], new[2].reshape(384, 1024), NN)
         for zz in range(4):
             for kk in range(2):
                 at = (2 * zz + kk) * 128
@@ -511,8 +526,10 @@
 
     def ring_send(kind, sign, step):
         part = halves[sign] if step == 0 else (0, 192)
-        links.send(ring[kind, sign] + step, r.at[chunk(kind, step, sign, part)],
-                   slot(kind, sign, step), dev_zp if sign > 0 else dev_zm)
+        device = dev_zp if sign > 0 else dev_zm
+        if kind == "far" and step == 3:
+            device = dev_yt_zp if sign > 0 else dev_yt_zm
+        links.send(ring[kind, sign] + step, r.at[chunk(kind, step, sign, part)], slot(kind, sign, step), device)
 
     def ring_recv(kind, sign, step):
         got = slot(kind, sign, step)
@@ -530,50 +547,63 @@
                 ring_add(kind, sign, step - 1)
             ring_send(kind, sign, step)
 
-    def ring_total(kind, i, rows_at):
+    def ring_total(kind):
         got = [ring_recv(kind, sign, 3)[...].astype(F32) for sign in (1, -1)]
-        return r[0, i, zhi, rows_at].astype(F32) + got[0] + got[1]
-
-    for i in range(4):
-        gate(i)
+        return got[0] + got[1]
+
+    n_finish(0)
+    gate(0)
+    gate(1)
+    n_onward(2, 1)
+    gate(2)
+    gate(3)
+    n_far(1)
     n_finish(1)
+    for i in (0, 2, 1, 3):
+        activate(i)
+    n_far(2)
+    n_finish(2)
     apply(0)
     apply(2)
+    apply(1)
     both_cores(0)
     y_send(0, (0,))
     ring_step("far", 0)
-    apply(1)
     both_cores(2)
     y_send(1, (0, 1))
     y_send(0, (1, 2))
     apply(3)
     both_cores(1)
     ring_step("own", 0)
+    links.drain(25, 12)
     y_add(0, (0,))
     ring_step("y", 0)
     y_send(1, (2, 3))
     y_send(0, (3,))
+    fin_id = links.ids()
+    links.send(fin_id, r.at[0, 0, zhi, hi], yfin, dev_yt)
     ring_step("far", 1)
     both_cores(3)
-    ring_step("own", 1)
+    links.drain(25, 12)
     y_add(1, (0, 1))
     ring_step("y", 1)
+    ring_step("own", 1)
     ring_step("far", 2)
+    y_add(0, (1, 2))
+    links.drain(25, 12)
+    ring_step("y", 2)
     ring_step("own", 2)
-    y_add(0, (1, 2))
-    ring_step("y", 2)
     ring_step("far", 3)
+    y_add(1, (2, 3))
+    links.drain(25, 10)
+    ring_step("y", 3)
     ring_step("own", 3)
-    y_add(1, (2, 3))
-    ring_step("y", 3)
     y_add(0, (3,))
-    fins[...] = ring_total("far", 0, hi).astype(BF16)
-    fin_id = links.ids()
-    links.send(fin_id, fins, yfin, dev_yt)
-    fin[...] = ring_total("own", 1, hi)
-    out_ref[lo, :] = ring_total("y", 1, lo).astype(BF16)
+    links.drain(25, 6)
     links.wait(fin_id, yfin, dev_yt)
-    out_ref[hi, :] = (fin[...] + yfin[...].astype(F32)).astype(BF16)
+    fin[...] = r[0, 1, zhi, hi].astype(F32) + yfin[...].astype(F32) + ring_total("far")
+    out_ref[hi, :] = (fin[...] + ring_total("own")).astype(BF16)
+    out_ref[lo, :] = (r[0, 1, zhi, lo].astype(F32) + ring_total("y")).astype(BF16)
     links.drain()
 
 
@@ -590,11 +620,11 @@
         V((2, 2, 48, 512), BF16), V((2, 2, 48, 512), BF16), V((2, 2, 48, 1024), BF16), V((2, 2, 48, 1024), BF16),
         V((2, 48, 1024), BF16), V((2, 48, 1024), BF16),
         V((3, 4, 2, 48, 1024), BF16),
-        V((4, 384, 384), F32), V((4, 2, 4, 384, 128), BF16), V((4, 4, 384, 128), BF16), V((2, 2, 4, 384, 128), BF16),
+        V((4, 384, 384), F32), V((4, 384, 384), BF16), V((4, 2, 4, 384, 128), BF16), V((4, 4, 384, 128), BF16), V((2, 2, 4, 384, 128), BF16),
         V((2, 4, 192, 128), BF16),
         V((6, 96, 128), BF16), V((6, 3, 192, 128), BF16),
-        V((192, 128), F32), V((192, 128), BF16), V((192, 128), BF16),
-        pltpu.SemaphoreType.DMA((N_SEM,)), pltpu.SemaphoreType.DMA((N_SEM,)), pltpu.SemaphoreType.DMA((8,)),
+        V((192, 128), F32), V((192, 128), BF16),
+        pltpu.SemaphoreType.DMA((N_SEND,)), pltpu.SemaphoreType.DMA((N_RECV,)), pltpu.SemaphoreType.DMA((7,)),
     ]
     return pl.pallas_call(
         kernel,

time: 103 us -> 98.9 us (0.960)
  Pallas kernels: 102 us -> 97.3 us
    pallas_call x1, Pallas kernels: 102 us -> 97.3 us  [on_device(): pl.pallas_call(kernel, out_shape=jax.ShapeDtypeStruct((384, 128), BF16),...]
where the time goes in v3:
time: 98.9 us; the launch traced here: 98.8 us
  Pallas kernels  97.3 us (98%)
  local copies, waits for them, and re-layouts  1.54 us (2%)
    pallas_call x1, Pallas kernels, on_device(): pl.pallas_call(kernel, out_shape=jax.ShapeDtypeStruct((384, 128), BF16),...  97.3 us

profile of v3, /device:TPU:8, one launch (start us, length us, event | category | flops | bytes accessed | tf_op | source)
XLA Modules:
  0.0 98.8 jit_solution(3623295642913279888)
XLA Ops:
  0.0 97.3 %ttt.1 = bf16[384,128]{1,0:T(8,128)(2,1)} custom-call(bf16[384,1024]{1,0:T(8,128)(2,1)} %key_ref.1, bf16[384,1024]{1,0:T(8,128)(2,1)} %val_ref.1, f32[384]{0:T(512)} %rate_ref.1, bf16[384,1024]{1,0:T(8,128)(2,1)} %qry_ref.1, bf16[32,1536]{1,0:T(8,128)(2,1)} %gate_ref.1, bf16[32,1536]{1,0:T(8,128)(2,1)} %up_ref.1, bf16[32,1536]{1,0:T(8,128)(2,1)} %bitcast.1), custom_call_target="tpu_custom_call" | custom-call | tf_op jit(solution)/shard_map/ttt/pallas_call | solution.py:629
  97.3 1.5 %copy.9 = bf16[384,128]{1,0:T(8,128)(2,1)} copy(bf16[384,128]{1,0:T(8,128)(2,1)} %ttt.1) | data formatting | bytes 196608

commit v4 on v3

--- a/solution.py
+++ b/solution.py
@@ -13,7 +13,8 @@
 NT = (((1,), (1,)), ((), ()))
 NN = (((1,), (0,)), ((), ()))
 F32, BF16 = jnp.float32, jnp.bfloat16
-N_SEND, N_RECV = 48, 171
+N_SEND, N_RECV = 32, 171
+LOW = 192
 
 
 def dot(a, b, dims):
@@ -60,7 +61,7 @@
 def kernel(key_ref, val_ref, rate_ref, qry_ref, gate_ref, up_ref, down_ref, out_ref,
            key_all, val_all, qry_all, rates, rate_row, raw, w, gp, uq, hid, grads,
            d, ry0, x1a0, x1b0, x2a0, x2b0, x1a, x1b, x2a, x2b, es, ry, new,
-           silu, act, ob, osib, r, ryo, slot0, slots, fin, yfin,
+           silu, act, ob, osib, r, ryo, slots, fin, yfin,
            send_sem, recv_sem, local_sem):
     c, s = lax.axis_index("ctx"), lax.axis_index("state")
     x, zlo, y = c // 8, (c // 4) % 2, c % 4
@@ -408,8 +409,8 @@
     direction(0, grads.at[0], key_all)
     cross_send(0)
     cross_send(1)
+    reduce_merge(2)
     cross_send(2)
-    reduce_merge(2)
     cross_send(3)
     links.drain(40, 25)
     reduce_merge(1)
@@ -470,7 +471,7 @@
 
     core_ids = links.ids(4)
     y_ids = {(i, j): links.ids() for i in range(2) for j in range(4)}
-    lo, hi = pl.ds(0, 192), pl.ds(192, 192)
+    lo, hi = pl.ds(0, LOW), pl.ds(LOW, 384 - LOW)
 
     def queries(i):
         b = block(yb if i % 2 else 1 - yb, zlo if i < 2 else 1 - zlo)
@@ -515,21 +516,26 @@
             r[i, 1, t, lo] = r[i, 1, t, lo] + ryo[i, t]
 
     def chunk(kind, step, sign, part):
-        base = 0 if kind == "y" else 192
+        base = 0 if kind == "y" else LOW
         return (step % 2, 0 if kind == "far" else 1, to(step, sign), pl.ds(base + part[0], part[1]))
 
-    halves = {1: (0, 96), -1: (96, 96)}
+    def span(kind, sign, step):
+        size = LOW if kind == "y" else 384 - LOW
+        if step:
+            return 0, size
+        return (0, size // 2) if sign > 0 else (size // 2, size // 2)
+
 
     def slot(kind, sign, step):
         n = 2 * streams.index(kind) + (0 if sign > 0 else 1)
-        return slot0.at[n] if step == 0 else slots.at[n, step - 1]
+        return slots.at[n, step, pl.ds(0, span(kind, sign, step)[1])]
 
     def ring_send(kind, sign, step):
-        part = halves[sign] if step == 0 else (0, 192)
         device = dev_zp if sign > 0 else dev_zm
         if kind == "far" and step == 3:
             device = dev_yt_zp if sign > 0 else dev_yt_zm
-        links.send(ring[kind, sign] + step, r.at[chunk(kind, step, sign, part)], slot(kind, sign, step), device)
+        links.send(ring[kind, sign] + step, r.at[chunk(kind, step, sign, span(kind, sign, step))],
+                   slot(kind, sign, step), device)
 
     def ring_recv(kind, sign, step):
         got = slot(kind, sign, step)
@@ -538,7 +544,7 @@
 
     def ring_add(kind, sign, step):
         got = ring_recv(kind, sign, step)
-        where = chunk(kind, step + 1, sign, halves[sign] if step == 0 else (0, 192))
+        where = chunk(kind, step + 1, sign, span(kind, sign, step))
         r[where] = r[where] + got[...]
 
     def ring_step(kind, step):
@@ -621,14 +627,13 @@
         V((2, 48, 1024), BF16), V((2, 48, 1024), BF16),
         V((3, 4, 2, 48, 1024), BF16),
         V((4, 384, 384), F32), V((4, 384, 384), BF16), V((4, 2, 4, 384, 128), BF16), V((4, 4, 384, 128), BF16), V((2, 2, 4, 384, 128), BF16),
-        V((2, 4, 192, 128), BF16),
-        V((6, 96, 128), BF16), V((6, 3, 192, 128), BF16),
-        V((192, 128), F32), V((192, 128), BF16),
+        V((2, 4, LOW, 128), BF16), V((6, 4, max(LOW, 384 - LOW), 128), BF16),
+        V((384 - LOW, 128), F32), V((384 - LOW, 128), BF16),
         pltpu.SemaphoreType.DMA((N_SEND,)), pltpu.SemaphoreType.DMA((N_RECV,)), pltpu.SemaphoreType.DMA((7,)),
     ]
     return pl.pallas_call(
         kernel,
-        out_shape=jax.ShapeDtypeStruct((384, 128), BF16),
+        out_shape=pltpu.VMEM((384, 128), BF16),
         in_specs=[any_spec, any_spec, any_spec, any_spec, any_spec, any_spec, any_spec],
         out_specs=vmem,
         scratch_shapes=scratch,

time: 98.9 us -> 97.2 us (0.983)
  no operation moved by 1% of the time
where the time goes in v4:
time: 97.2 us
  Pallas kernels  96.5 us (99%)
    pallas_call x1, Pallas kernels, on_device(): pl.pallas_call(kernel, out_shape=pltpu.VMEM((384, 128), BF16), in_specs=[...  96.5 us

profile of v4, /device:TPU:8, one launch (start us, length us, event | category | flops | bytes accessed | tf_op | source)
XLA Modules:
  0.0 97.2 jit_solution(3353014260917101172)
XLA Ops:
  0.0 96.5 %ttt.1 = bf16[384,128]{1,0:T(8,128)(2,1)S(1)} custom-call(bf16[384,1024]{1,0:T(8,128)(2,1)} %key_ref.1, bf16[384,1024]{1,0:T(8,128)(2,1)} %val_ref.1, f32[384]{0:T(512)} %rate_ref.1, bf16[384,1024]{1,0:T(8,128)(2,1)} %qry_ref.1, bf16[32,1536]{1,0:T(8,128)(2,1)} %gate_ref.1, bf16[32,1536]{1,0:T(8,128)(2,1)} %up_ref.1, bf16[32,1536]{1,0:T(8,128)(2,1)} %bitcast.1), custom_call_target="tpu_custom_call" | custom-call | tf_op jit(solution)/shard_map/ttt/pallas_call | solution.py:634
  96.5 0.6 copy.9

commit v5 on v4

--- a/solution.py
+++ b/solution.py
@@ -13,7 +13,7 @@
 NT = (((1,), (1,)), ((), ()))
 NN = (((1,), (0,)), ((), ()))
 F32, BF16 = jnp.float32, jnp.bfloat16
-N_SEND, N_RECV = 32, 171
+N_SEND, N_RECV = 24, 145
 LOW = 192
 
 
@@ -170,13 +170,16 @@
         for kind in kinds:
             links.wait(sib_ids[i, kind], rows(i, blocks[kind], (0, 192), 1 - k), dev_core)
 
-    def gather(late, piece, half):
-        ids = {}
+    gather_ids = {}
+
+    def gather(late, piece, half, turn=(0, 1, 2, 3)):
+        ids = gather_ids
 
         def at(name, j):
-            if (name, j) not in ids:
-                ids[name, j] = links.ids()
-            return ids[name, j]
+            key = (name, turn[j])
+            if key not in ids:
+                ids[key] = links.ids()
+            return ids[key]
 
         def move(name, j, ref, device):
             links.send(at(name, j), ref, ref, device)
@@ -442,7 +445,7 @@
     def n_half(a, xx, other, h):
         return new.at[a, xx, po if other else p, :, ab[h]]
 
-    n_start, n_start_y, n_cross, n_onward, n_far, n_finish = gather((0,), n_piece, n_half)
+    n_start, n_start_y, n_cross, n_onward, n_far, n_finish = gather((0,), n_piece, n_half, (2, 0, 1))
     links.drain(25, 25)
     reduce_finish(2)
     n_start(2)

time: 97.2 us -> 96.9 us (level)
  no operation moved by 1% of the time
where the time goes in v5:
time: 96.9 us
  Pallas kernels  96.2 us (99%)
    pallas_call x1, Pallas kernels, on_device(): pl.pallas_call(kernel, out_shape=pltpu.VMEM((384, 128), BF16), in_specs=[...  96.2 us

profile of v5, /device:TPU:8, one launch (start us, length us, event | category | flops | bytes accessed | tf_op | source)
XLA Modules:
  0.0 96.9 jit_solution(17373195219231253418)
XLA Ops:
  0.0 96.2 %ttt.1 = bf16[384,128]{1,0:T(8,128)(2,1)S(1)} custom-call(bf16[384,1024]{1,0:T(8,128)(2,1)} %key_ref.1, bf16[384,1024]{1,0:T(8,128)(2,1)} %val_ref.1, f32[384]{0:T(512)} %rate_ref.1, bf16[384,1024]{1,0:T(8,128)(2,1)} %qry_ref.1, bf16[32,1536]{1,0:T(8,128)(2,1)} %gate_ref.1, bf16[32,1536]{1,0:T(8,128)(2,1)} %up_ref.1, bf16[32,1536]{1,0:T(8,128)(2,1)} %bitcast.1), custom_call_target="tpu_custom_call" | custom-call | tf_op jit(solution)/shard_map/ttt/pallas_call | solution.py:637
  96.2 0.6 copy.9
